TPU v7x, 256 devices: a whole 4x4x8 slice. The times are simulated.
256 devices in a mesh: rep: 8 (over z_hi, core), seq: 16 (over y, x), chip: 2 (over z_lo).
Axes of the slice: x: 4, y: 4, z: 8 (z_hi: 4, z_lo: 2; z = z_hi * 2 + z_lo), core: 2. Of those that a mesh axis runs over, the one named last changes fastest.
Arguments:
- text_rows: bfloat16 [2048, 3072], P('rep', 'seq'), may hold values from -60 to 60
- modulation: float32 [50, 2, 3072], P(None, None, 'seq'), may hold values from -3 to 3
- timestep: int32 [8], replicated, may hold values from 0 to 49
- row_request: int32 [2048, 1], P('rep'), may hold values from 0 to 7; in each aligned block of 16 rows (0 to 15, 16 to 31, ...) at most 4 rows name the same one
- w_key: bfloat16 [3072, 3072], P('seq', 'chip'), may hold values from -0.109375 to 0.109375
- w_value: bfloat16 [3072, 3072], P('seq', 'chip'), may hold values from -0.4375 to 0.4375
- q_image: bfloat16 [8, 1792, 3072], P('rep', ('seq', 'chip')), may hold values from -56 to 56
- k_image: bfloat16 [8, 1792, 3072], P('rep', ('seq', 'chip')), may hold values from -16 to 16
- v_image: bfloat16 [8, 1792, 3072], P('rep', ('seq', 'chip')), may hold values from -24 to 24
Outputs:
- attended: bfloat16 [8, 1792, 3072], P('rep', ('seq', 'chip'))
Inputs may be any that keep to these rules, and one draw needn't show every extreme that they name: `row_request`: in each aligned block of 16 rows no request is named by more than 4 rows; every request is named by some row.
All inputs are finite; a program needn't handle non-finite values.
Results may differ from a plain program's by a relative error of at most 0.025.
Values may be sent and summed in bfloat16 or wider, within the bound.
A program may use at most 128 MiB of HBM per device.

v0:
```python
import math

import jax
import jax.numpy as jnp
from jax import lax
from jax.sharding import PartitionSpec as P

D = 3072
HEADS = 24
HEAD_DIM = 128
CAP = 4


def block_update(carry, query, keys, values, is_live):
    maximum, total, mixed = carry
    heads = maximum.shape[0]
    head_dim = query.shape[2]
    keyed = keys.reshape(keys.shape[0], heads, head_dim)
    valued = values.reshape(values.shape[0], heads, head_dim)
    scores = jnp.einsum("qhd,khd->hqk", query, keyed, preferred_element_type=jnp.float32) * (
        1.0 / math.sqrt(head_dim)
    )
    if is_live is not None:
        scores = jnp.where(is_live[None, None, :], scores, -jnp.inf)
    newest = jnp.maximum(maximum, jnp.max(scores, axis=2))
    factor = jnp.exp(maximum - newest)
    weights = jnp.exp(scores - newest[:, :, None])
    total = total * factor + jnp.sum(weights, axis=2)
    mixed = mixed * factor[:, :, None] + jnp.einsum(
        "hqk,khd->hqd", weights.astype(jnp.bfloat16), valued, preferred_element_type=jnp.float32
    )
    return (newest, total, mixed)


def start_carry(heads, count):
    return (
        jnp.full((heads, count), -jnp.inf, jnp.float32),
        jnp.zeros((heads, count), jnp.float32),
        jnp.zeros((heads, count, HEAD_DIM), jnp.float32),
    )


def finish(carry):
    maximum, total, mixed = carry
    result = mixed / total[:, :, None]
    return result.transpose(1, 0, 2).reshape(result.shape[1], -1).astype(jnp.bfloat16)


def local(text_rows, modulation, timestep, row_request, w_key, w_value, q_image, k_image, v_image):
    block_rows = text_rows.shape[0]
    values_text = text_rows.astype(jnp.float32)
    row_sum, row_square = lax.psum(
        (jnp.sum(values_text, axis=1), jnp.sum(values_text * values_text, axis=1)), "seq"
    )
    row_mean = row_sum / D
    row_power = row_square / D
    request = row_request[:, 0]
    group_count = timestep.shape[0]
    groups = jnp.arange(group_count, dtype=jnp.int32)
    steps_count = modulation.shape[0]
    pick_request = (request[:, None] == groups[None, :]).astype(jnp.float32)
    pick_step = (timestep[:, None] == jnp.arange(steps_count, dtype=jnp.int32)[None, :]).astype(
        jnp.float32
    )
    row_step = jnp.dot(pick_request, pick_step, precision=lax.Precision.HIGHEST)
    table = modulation.reshape(steps_count, -1)
    shifts = jnp.dot(row_step, table, precision=lax.Precision.HIGHEST).reshape(block_rows, 2, -1)
    normed = (values_text - row_mean[:, None]) * lax.rsqrt(
        row_power[:, None] - row_mean[:, None] * row_mean[:, None] + 1e-06
    )
    shaped = (normed * (1.0 + shifts[:, 1]) + shifts[:, 0]).astype(jnp.bfloat16)
    w_both = jnp.concatenate([w_key, w_value], axis=1)
    own_count = block_rows // lax.axis_size("seq")
    projected = lax.psum_scatter(
        jnp.dot(shaped, w_both, preferred_element_type=jnp.float32).astype(jnp.bfloat16),
        "seq",
        scatter_dimension=0,
        tiled=True,
    ).astype(jnp.float32)
    half_width = w_key.shape[1]
    key_rows = projected[:, :half_width].astype(jnp.bfloat16)
    value_rows = projected[:, half_width:].astype(jnp.bfloat16)
    offset = lax.axis_index("seq") * own_count
    target = lax.dynamic_slice_in_dim(request, offset, own_count, 0)
    order_index = jnp.arange(own_count, dtype=jnp.int32)
    earlier = (target[None, :] == target[:, None]) & (order_index[None, :] < order_index[:, None])
    slot = jnp.sum(earlier.astype(jnp.int32), axis=1)
    place = target * CAP + slot
    positions = jnp.arange(group_count * CAP, dtype=jnp.int32)
    matches = positions[:, None] == place[None, :]
    placing = matches.astype(jnp.bfloat16)
    send_keys = (
        jnp.dot(placing, key_rows, preferred_element_type=jnp.float32)
        .astype(jnp.bfloat16)
        .reshape(group_count, CAP, half_width)
    )
    send_values = (
        jnp.dot(placing, value_rows, preferred_element_type=jnp.float32)
        .astype(jnp.bfloat16)
        .reshape(group_count, CAP, half_width)
    )
    send_flags = jnp.sum(matches.astype(jnp.int32), axis=1).reshape(group_count, CAP)
    got_keys, got_values, got_flags = (
        lax.all_to_all(send_keys, "rep", split_axis=0, concat_axis=0, tiled=True),
        lax.all_to_all(send_values, "rep", split_axis=0, concat_axis=0, tiled=True),
        lax.all_to_all(send_flags, "rep", split_axis=0, concat_axis=0, tiled=True),
    )
    got_keys = got_keys.reshape(-1, half_width)
    got_values = got_values.reshape(-1, half_width)
    got_flags = got_flags.reshape(-1)
    slot_keys, slot_values, slot_flags = (
        lax.all_gather(got_keys, "seq", axis=0, tiled=True),
        lax.all_gather(got_values, "seq", axis=0, tiled=True),
        lax.all_gather(got_flags, "seq", axis=0, tiled=True),
    )
    is_live = slot_flags > 0
    text_keys, text_values = (
        lax.all_gather(slot_keys, "chip", axis=1, tiled=True),
        lax.all_gather(slot_values, "chip", axis=1, tiled=True),
    )
    query_rows = q_image[0]
    query = query_rows.reshape(query_rows.shape[0], HEADS, HEAD_DIM)
    carry = block_update(
        start_carry(HEADS, query_rows.shape[0]), query, text_keys, text_values, is_live
    )
    carry = block_update(
        carry,
        query,
        lax.all_gather(k_image[0], ("seq", "chip"), axis=0, tiled=True),
        lax.all_gather(v_image[0], ("seq", "chip"), axis=0, tiled=True),
        None,
    )
    attended = finish(carry)
    return attended[None]


def solution(mesh):
    return jax.shard_map(
        local,
        mesh=mesh,
        in_specs=(
            P("rep", "seq"),
            P(None, None, "seq"),
            P(),
            P("rep", None),
            P("seq", "chip"),
            P("seq", "chip"),
            P("rep", ("seq", "chip"), None),
            P("rep", ("seq", "chip"), None),
            P("rep", ("seq", "chip"), None),
        ),
        out_specs=P("rep", ("seq", "chip"), None),
        check_vma=False,
    )
```

profile of v0, /device:TPU:1, one launch (start us, length us, event | category | flops | bytes accessed | tf_op | source)
XLA Modules:
  0.0 877.8 jit_solution(14627613407159670947)
XLA Ops:
  10.1 34.3 %all-reduce.1 = (f32[256]{0:T(256)S(1)}, f32[256]{0:T(256)S(1)}) all-reduce(f32[256]{0:T(256)S(1)} %get-tuple-element.6, f32[256]{0:T(256)S(1)} %get-tuple-element.5), channel_id=1, replica_groups=mesh['rep'=8,'seq'=16,'chip'=2] {'seq'}, use_global_device_ids=true, to_apply=%region_5.0 | all-reduce | flops 512 | bytes 4096 | tf_op jit(solution)/shard_map/psum | solution.py:52
  44.4 3.1 convolution_convert_fusion
  47.9 81.9 %reduce-scatter.2.cloned.1.call-done = bf16[16,3072]{1,0:T(8,128)(2,1)} async-done(((bf16[256,3072]{1,0:T(8,128)(2,1)}), bf16[16,3072]{1,0:T(8,128)(2,1)}) %reduce-scatter.2.cloned.1.call-update) | async-done | bytes 98320 | tf_op jit(solution)/shard_map/reduce_scatter | solution.py:74
  130.9 16.7 %all_to_all.19 = bf16[8,4,1536]{2,1,0:T(4,128)(2,1)S(1)} all-to-all(bf16[8,4,1536]{2,1,0:T(4,128)(2,1)S(1)} %reshape.101), channel_id=1, replica_groups=mesh['rep'=8,'seq'=16,'chip'=2] {'rep'}, dimensions={0} | all-to-all | bytes 196608 | tf_op jit(solution)/shard_map/all_to_all | solution.py:104
  149.5 11.3 %all_to_all.20 = bf16[8,4,1536]{2,1,0:T(4,128)(2,1)S(1)} all-to-all(bf16[8,4,1536]{2,1,0:T(4,128)(2,1)S(1)} %reshape.104), channel_id=1, replica_groups=mesh['rep'=8,'seq'=16,'chip'=2] {'rep'}, dimensions={0} | all-to-all | bytes 196608 | tf_op jit(solution)/shard_map/all_to_all | solution.py:105
  161.5 30.2 %all-gather.9.cloned.1.call-done = bf16[512,1536]{1,0:T(8,128)(2,1)} async-done(((bf16[32,1536]{1,0:T(8,128)(2,1)}), bf16[512,1536]{1,0:T(8,128)(2,1)}) %all-gather.9.cloned.1.call-update) | async-done | bytes 1572880 | tf_op jit(solution)/shard_map/all_gather | solution.py:112
  191.8 50.8 %all-gather.13.cloned.1.call-done = bf16[512,1536]{1,0:T(8,128)(2,1)} async-done(((bf16[32,1536]{1,0:T(8,128)(2,1)}), bf16[512,1536]{1,0:T(8,128)(2,1)}) %all-gather.13.cloned.1.call-update) | async-done | bytes 1572880 | tf_op jit(solution)/shard_map/all_gather | solution.py:113
  244.7 8.6 all-to-all-start
  254.8 5.5 all-to-all-done
  261.7 11.3 %all-reduce = s32[512]{0:T(512)S(1)} all-reduce(s32[512]{0:T(512)S(1)} %dynamic-update-slice), channel_id=1, replica_groups=mesh['rep'=8,'seq'=16,'chip'=2] {'seq'}, use_global_device_ids=true, to_apply=%add | all-reduce | flops 512 | bytes 4096
  273.1 21.7 %all-gather.11.cloned.1.call-done = bf16[512,3072]{1,0:T(8,128)(2,1)} async-done(((bf16[512,1536]{1,0:T(8,128)(2,1)}), bf16[512,3072]{1,0:T(8,128)(2,1)}) %all-gather.11.cloned.1.call-update) | async-done | bytes 3145744 | tf_op jit(solution)/shard_map/all_gather | solution.py:118
  294.7 3.2 copy.51
  297.9 49.0 %all-gather.15.cloned.1.call-done = bf16[512,3072]{1,0:T(8,128)(2,1)} async-done(((bf16[512,1536]{1,0:T(8,128)(2,1)}), bf16[512,3072]{1,0:T(8,128)(2,1)}) %all-gather.15.cloned.1.call-update) | async-done | bytes 3145744 | tf_op jit(solution)/shard_map/all_gather | solution.py:119
  346.9 4.7 copy.54
  352.3 1.5 copy-done.1
  354.6 241.0 %all-gather.17.cloned.1.call-done = bf16[1,1792,3072]{2,1,0:T(8,128)(2,1)} async-done(((bf16[1,56,3072]{2,1,0:T(8,128)(2,1)}), bf16[1,1792,3072]{2,1,0:T(8,128)(2,1)}) %all-gather.17.cloned.1.call-update) | async-done | bytes 11010064 | tf_op jit(solution)/shard_map/all_gather | solution.py:129
  595.6 13.9 %copy.56 = bf16[1,1792,3072]{1,2,0:T(8,128)(2,1)} copy(bf16[1,1792,3072]{2,1,0:T(8,128)(2,1)} %all-gather.17.cloned.1.call-done) | data formatting | bytes 22020096 | tf_op jit(solution)/shard_map/all_gather | solution.py:129
  609.5 5.3 multiply_reduce_fusion
  614.8 3.7 copy-done
  618.5 1.7 fusion
  620.2 221.4 %all-gather.19.cloned.1.call-done = bf16[1,1792,3072]{2,1,0:T(8,128)(2,1)} async-done(((bf16[1,56,3072]{2,1,0:T(8,128)(2,1)}), bf16[1,1792,3072]{2,1,0:T(8,128)(2,1)}) %all-gather.19.cloned.1.call-update) | async-done | bytes 11010064 | tf_op jit(solution)/shard_map/all_gather | solution.py:130
  841.6 14.0 %copy.59 = bf16[1,1792,3072]{1,2,0:T(8,128)(2,1)} copy(bf16[1,1792,3072]{2,1,0:T(8,128)(2,1)} %all-gather.19.cloned.1.call-done) | data formatting | bytes 22020096 | tf_op jit(solution)/shard_map/all_gather | solution.py:130
  855.6 10.9 %fusion.15 = f32[56,24,128]{2,0,1:T(8,128)S(1)} fusion(bf16[1792,24,128]{0,2,1:T(8,128)(2,1)} %bitcast.92, f32[24,56,1792]{2,1,0:T(8,128)} %copy-done, f32[24,56]{1,0:T(8,128)S(1)} %max.18), kind=kOutput, calls=%fused_computation.21 | convolution fusion | flops 623788032 | bytes 21337344 | tf_op jit(solution)/shard_map/hqk,khd->hqd/dot_general | solution.py:29
  866.6 3.4 fusion.36
  (55 shorter events, 14.4 us)
Async XLA Ops:
  6.5 41.0 %copy-start.4 = (s32[256,1]{0,1:T(1,128)S(1)}, s32[256,1]{0,1:T(1,128)}, u32[]{:S(2)}) copy-start(s32[256,1]{0,1:T(1,128)} %param.12) | copy-start | bytes 3076
  6.5 123.3 %reduce-scatter.2.cloned.1.call-start = ((), (), s32[]{:S(2)}) async-start(), calls=%async_computation.4 | async-start | bytes 1671168 | tf_op jit(solution)/shard_map/reduce_scatter | solution.py:74
  47.5 205.8 %copy-start.3 = (bf16[1,56,3072]{2,1,0:T(8,128)(2,1)S(1)}, bf16[1,56,3072]{2,1,0:T(8,128)(2,1)}, u32[]{:S(2)}) copy-start(bf16[1,56,3072]{2,1,0:T(8,128)(2,1)} %param.15) | copy-start | bytes 1032196
  47.5 205.9 %copy-start.5 = (u32[256]{0:T(256)S(1)}, u32[256]{0:T(256)}, u32[]{:S(2)}) copy-start(u32[256]{0:T(256)} %constant.39) | copy-start | bytes 3076
  47.5 144.2 %all-gather.9.cloned.1.call-start = ((), (), s32[]{:S(2)}) async-start(), calls=%async_computation.5 | async-start | bytes 1671168 | tf_op jit(solution)/shard_map/all_gather | solution.py:112
  148.4 94.2 %all-gather.13.cloned.1.call-start = ((), (), s32[]{:S(2)}) async-start(), calls=%async_computation.7 | async-start | bytes 1671168 | tf_op jit(solution)/shard_map/all_gather | solution.py:113
  161.5 133.3 %all-gather.11.cloned.1.call-start = ((), (), s32[]{:S(2)}) async-start(), calls=%async_computation.6 | async-start | bytes 4718592 | tf_op jit(solution)/shard_map/all_gather | solution.py:118
  191.8 155.1 %all-gather.15.cloned.1.call-start = ((), (), s32[]{:S(2)}) async-start(), calls=%async_computation.8 | async-start | bytes 4718592 | tf_op jit(solution)/shard_map/all_gather | solution.py:119
  242.6 353.0 %all-gather.17.cloned.1.call-start = ((), (), s32[]{:S(2)}) async-start(), calls=%async_computation.9 | async-start | bytes 11354112 | tf_op jit(solution)/shard_map/all_gather | solution.py:129
  243.2 598.4 %all-gather.19.cloned.1.call-start = ((), (), s32[]{:S(2)}) async-start(), calls=%async_computation.10 | async-start | bytes 11354112 | tf_op jit(solution)/shard_map/all_gather | solution.py:130
  244.7 15.5 %all-to-all-start = ((s32[8,1,4]{2,1,0:T(1,128)}), s32[8,1,4]{2,1,0:T(1,128)S(1)}, u32[]{:S(2)}, u32[]{:S(2)}) async-start(s32[8,1,4]{2,1,0:T(1,128)} %bitcast.1), calls=%async_computation | async-start | bytes 8192 | tf_op jit(solution)/shard_map/all_to_all | solution.py:106
  352.3 1.6 copy-start.1
  614.8 3.7 copy-start
  855.6 10.9 %copy-start.2 = (f32[24,512,56]{1,2,0:T(8,128)S(1)}, f32[24,512,56]{1,2,0:T(8,128)}, u32[]{:S(2)}) copy-start(f32[24,512,56]{1,2,0:T(8,128)} %copy-done.1) | copy-start | bytes 8257540
Sparse Core Ops, SparseCore 0:
  47.6 82.1 reduce-scatter.1
  148.5 43.2 all-gather.8
  194.2 48.3 all-gather.12
  244.3 50.4 all-gather.10
  296.4 50.4 all-gather.14
  348.5 247.0 all-gather.16
  597.4 244.1 all-gather.18
where the time goes:
time: 879 us; the launch traced here: 878 us
  waiting for transfers between devices  703 us (80%)
  blocking collectives  73.6 us (8%)
  local copies, waits for them, and re-layouts  46.7 us (5%)
  matrix products  27 us (3%)
  between operations  14.4 us (2%)
  starting transfers between devices  8.86 us (1%)
    all_gather x1, waiting for transfers between devices, local(): lax.all_gather(k_image[0], ('seq', 'chip'), axis=0, tiled=True)  241 us
    all_gather x1, waiting for transfers between devices, local(): lax.all_gather(v_image[0], ('seq', 'chip'), axis=0, tiled=True)  221 us
    reduce_scatter x1, waiting for transfers between devices, local(): lax.psum_scatter(jnp.dot(shaped, w_both, preferred_element_type=jnp.float...  81.9 us
    all_gather x1, waiting for transfers between devices, local(): lax.all_gather(got_values, 'seq', axis=0, tiled=True)  50.8 us
    all_gather x1, waiting for transfers between devices, local(): lax.all_gather(slot_values, 'chip', axis=1, tiled=True)  49 us
    psum x1, blocking collectives, local(): lax.psum((jnp.sum(values_text, axis=1), jnp.sum(values_text * values_text...  34.3 us
    all_gather x1, waiting for transfers between devices, local(): lax.all_gather(got_keys, 'seq', axis=0, tiled=True)  30.2 us
    all_gather x1, waiting for transfers between devices, local(): lax.all_gather(slot_keys, 'chip', axis=1, tiled=True)  21.7 us
  transfers between devices with their start and end apart: 8, of which 8 were waited for; matrix products, arithmetic and copies ran while one was open for 4% of the time, Pallas kernels for 0%

commit v1 on v0

v1 whole, which is shorter than its diff:
```python
import functools
import math

import jax
import jax.numpy as jnp
from jax import lax
from jax.experimental import pallas as pl
from jax.experimental.pallas import tpu as pltpu
from jax.sharding import PartitionSpec as P

D = 3072
HEAD_DIM = 128
CAP = 4
BLOCK = 16
NX = 4
NY = 4
NZ = 2
REPS = 8
GROUPS = NY * NZ
WIDE = D // GROUPS
HEADS = WIDE // HEAD_DIM
IMG_DEV = 56
CHUNK = GROUPS * IMG_DEV
ROWS = 256
QUARTER = ROWS // NX
SLOTS = QUARTER // BLOCK * CAP
TEXT = REPS * SLOTS
PACKED = 2 * WIDE + 128
FACTOR = math.log2(math.e) / math.sqrt(HEAD_DIM)
LOWEST = -1e30
MESH = pl.DeviceIdType.MESH

S_TEXT, S_MOD, S_WK, S_WV = 0, 4, 8, 12
S_Q, S_K, S_V = 16, 24, 32
S_KX, S_VX, S_STAT, S_SUM = 40, 44, 48, 52
S_REP, S_TX, S_OUT = 56, 64, 68
S_ALL = 76


def kernel(
    text, mod, step, req, w_key, w_value, q_in, k_in, v_in, out,
    tx, md, wk, wv, qb, kvb, stat_s, stat_r, acc, sum_s, sum_r, rep_s, txt, qh, m, l, o, o_s,
    ssem, rsem, lsem,
):
    f32, bf16 = jnp.float32, jnp.bfloat16
    rep, seq, z = lax.axis_index("rep"), lax.axis_index("seq"), lax.axis_index("chip")
    y, x = lax.div(seq, NX), lax.rem(seq, NX)
    gi = z * NY + y

    def group_peer(d):
        t = lax.rem(gi + d, GROUPS)
        return (rep, lax.rem(t, NY) * NX + x, lax.div(t, NY))

    def x_peer(d):
        return (rep, y * NX + lax.rem(x + d, NX), z)

    def y_peer(d):
        return (rep, lax.rem(y + d, NY) * NX + x, z)

    def rep_peer(d):
        return (lax.rem(rep + d, REPS), seq, z)

    def columns(index):
        return pl.ds(pl.multiple_of(index * WIDE, WIDE), WIDE)

    def remote(src, dst, index, peer):
        return pltpu.make_async_remote_copy(
            src_ref=src, dst_ref=dst, send_sem=ssem.at[index], recv_sem=rsem.at[index],
            device_id=peer, device_id_type=MESH,
        )

    barrier = pltpu.get_barrier_semaphore()
    peers = (
        [group_peer(d) for d in range(1, GROUPS)]
        + [x_peer(d) for d in range(1, NX)]
        + [rep_peer(d) for d in range(1, REPS)]
    )
    for peer in peers:
        pl.semaphore_signal(barrier, inc=1, device_id=peer, device_id_type=MESH)

    own = [
        pltpu.make_async_copy(k_in.at[0, :, columns(gi)], kvb.at[0, 0, 0], lsem.at[0]),
        pltpu.make_async_copy(v_in.at[0, :, columns(gi)], kvb.at[0, 1, 0], lsem.at[1]),
        pltpu.make_async_copy(q_in.at[0, :, columns(gi)], qb.at[0], lsem.at[2]),
        pltpu.make_async_copy(w_key.at[:, columns(y)], wk.at[0], lsem.at[3]),
        pltpu.make_async_copy(w_value.at[:, columns(y)], wv.at[0], lsem.at[4]),
    ]
    for copy in own:
        copy.start()
    for g in range(REPS):
        md[0, 2 * g : 2 * g + 2, :] = mod[step[g]]

    pl.semaphore_wait(barrier, len(peers))

    sent = []

    def send(src, dst, index, peer):
        copy = remote(src, dst, index, peer)
        copy.start()
        sent.append(copy)
        return copy

    got_text = [send(text, tx.at[d], S_TEXT + d, y_peer(d)) for d in range(1, NY)]
    got_mod = [send(md.at[0], md.at[d], S_MOD + d, y_peer(d)) for d in range(1, NY)]
    got_k, got_v, got_q, got_w = [], [], [], []
    for d in range(1, GROUPS):
        there = columns(lax.rem(gi + d, GROUPS))
        got_k.append(send(k_in.at[0, :, there], kvb.at[0, 0, d], S_K + d, group_peer(d)))
        got_v.append(send(v_in.at[0, :, there], kvb.at[0, 1, d], S_V + d, group_peer(d)))
    for d in range(1, NY):
        there = columns(lax.rem(y + d, NY))
        got_w.append(send(w_key.at[:, there], wk.at[d], S_WK + d, y_peer(d)))
        got_w.append(send(w_value.at[:, there], wv.at[d], S_WV + d, y_peer(d)))
    for d in range(1, GROUPS):
        there = columns(lax.rem(gi + d, GROUPS))
        got_q.append(send(q_in.at[0, :, there], qb.at[d], S_Q + d, group_peer(d)))

    for copy in got_text:
        copy.wait_recv()

    def text_part(d):
        return (text[...] if d == 0 else tx[d]).astype(f32)

    total, square = None, None
    for d in range(NY):
        part = text_part(d)
        total = part if total is None else total + part
        square = part * part if square is None else square + part * part
    lane = lax.broadcasted_iota(jnp.int32, (ROWS, 128), 1)
    both = jnp.where(
        lane == 0,
        jnp.sum(total, axis=1, keepdims=True),
        jnp.where(lane == 1, jnp.sum(square, axis=1, keepdims=True), 0.0),
    )
    stat_s[...] = both.T[0:8]
    got_stat = [send(stat_s, stat_r.at[d], S_STAT + d, x_peer(d)) for d in range(1, NX)]

    own[0].wait()
    for copy in got_k:
        copy.wait_recv()
    k_right = send(kvb.at[0, 0], kvb.at[1, 0], S_KX + 1, x_peer(1))
    own[1].wait()
    for copy in got_v:
        copy.wait_recv()
    v_left = send(kvb.at[0, 1], kvb.at[3, 1], S_VX + 3, x_peer(3))
    v_right = send(kvb.at[0, 1], kvb.at[1, 1], S_VX + 1, x_peer(1))
    k_left = send(kvb.at[0, 0], kvb.at[3, 0], S_KX + 3, x_peer(3))

    for copy in got_stat:
        copy.wait_recv()
    summed = stat_s[...] + stat_r[1] + stat_r[2] + stat_r[3]
    stats = jnp.concatenate([summed, jnp.zeros((120, ROWS), f32)], axis=0).T
    mean = stats[:, 0:1] / D
    power = stats[:, 1:2] / D
    scaled = lax.rsqrt(power - mean * mean + 1e-06)
    request = req[...]
    lane16 = lax.broadcasted_iota(jnp.int32, (ROWS, 2 * REPS), 1)
    pick_shift = (lane16 == 2 * request).astype(f32)
    pick_scale = (lane16 == 2 * request + 1).astype(f32)
    for copy in got_mod:
        copy.wait_recv()
    for copy in got_w:
        copy.wait_recv()
    own[3].wait()
    own[4].wait()
    for d in range(NY):
        picked = md[d]
        shift = jnp.dot(pick_shift, picked, precision=lax.Precision.HIGHEST, preferred_element_type=f32)
        scale = jnp.dot(pick_scale, picked, precision=lax.Precision.HIGHEST, preferred_element_type=f32)
        shaped = ((text_part(d) - mean) * scaled * (1.0 + scale) + shift).astype(bf16)
        key_part = jnp.dot(shaped, wk[d], preferred_element_type=f32)
        value_part = jnp.dot(shaped, wv[d], preferred_element_type=f32)
        if d == 0:
            acc[:, 0:WIDE] = key_part
            acc[:, WIDE : 2 * WIDE] = value_part
        else:
            acc[:, 0:WIDE] += key_part
            acc[:, WIDE : 2 * WIDE] += value_part
    sum_s[...] = acc[...].astype(bf16)
    got_sum = []
    for d in range(1, NX):
        quarter = pl.ds(pl.multiple_of(lax.rem(x + d, NX) * QUARTER, QUARTER), QUARTER)
        got_sum.append(send(sum_s.at[quarter], sum_r.at[d], S_SUM + d, x_peer(d)))

    quarter = pl.ds(pl.multiple_of(x * QUARTER, QUARTER), QUARTER)
    target = req[quarter, :]
    lane = lax.broadcasted_iota(jnp.int32, (QUARTER, 128), 1)
    is_target = lane == target
    earlier = (
        lax.broadcasted_iota(jnp.int32, (QUARTER, QUARTER), 1)
        < lax.broadcasted_iota(jnp.int32, (QUARTER, QUARTER), 0)
    ).astype(f32).astype(bf16)
    count = jnp.dot(earlier, is_target.astype(f32).astype(bf16), preferred_element_type=f32)
    slot = jnp.sum(jnp.where(is_target, count, 0.0), axis=1, keepdims=True).astype(jnp.int32)
    placing = (lane == target * SLOTS + slot).astype(f32).astype(bf16)

    for copy in got_sum:
        copy.wait_recv()
    rows = acc[quarter, :] + sum_r[1].astype(f32) + sum_r[2].astype(f32) + sum_r[3].astype(f32)
    rows = jnp.concatenate([rows.astype(bf16), jnp.ones((QUARTER, 128), bf16)], axis=1)
    packed = lax.dot_general(placing, rows, (((0,), (0,)), ((), ())), preferred_element_type=f32)
    rep_s[...] = packed.astype(bf16).reshape(REPS, SLOTS, PACKED)
    got_rep = [
        send(rep_s.at[lax.rem(rep + d, REPS)], txt.at[0, d], S_REP + d, rep_peer(d))
        for d in range(1, REPS)
    ]
    txt[0, 0] = rep_s[rep]

    def load_rows(ref, cols):
        block = ref[:, :, cols].astype(f32)
        return block.reshape(CHUNK, HEAD_DIM).astype(bf16)

    def update(h, keys, values, live):
        cols = pl.ds(pl.multiple_of(h * HEAD_DIM, HEAD_DIM), HEAD_DIM)
        s = lax.dot_general(qh[:, cols], keys, (((1,), (1,)), ((), ())), preferred_element_type=f32)
        if live is not None:
            s = jnp.where(live, s, LOWEST)
        before = m[h]
        newest = jnp.maximum(before, jnp.max(s, axis=1, keepdims=True))
        weights = jnp.exp2((s - newest[:, 0:1]) * FACTOR)
        fade = jnp.exp2((before - newest) * FACTOR)
        m[h] = newest
        l[h] = l[h] * fade + jnp.sum(weights, axis=1, keepdims=True)
        o[h] = o[h] * fade + jnp.dot(weights.astype(bf16), values, preferred_element_type=f32)

    def image_chunk(index):
        def one(h, carry):
            cols = pl.ds(pl.multiple_of(h * HEAD_DIM, HEAD_DIM), HEAD_DIM)
            update(h, load_rows(kvb.at[index, 0], cols), load_rows(kvb.at[index, 1], cols), None)
            return carry

        lax.fori_loop(0, HEADS, one, 0)

    m[...] = jnp.full(m.shape, LOWEST, f32)
    l[...] = jnp.zeros(l.shape, f32)
    o[...] = jnp.zeros(o.shape, f32)

    k_right.wait_recv()
    k_far = send(kvb.at[1, 0], kvb.at[2, 0], S_KX + 2, x_peer(1))
    v_left.wait_recv()
    v_far = send(kvb.at[3, 1], kvb.at[2, 1], S_VX + 2, x_peer(3))

    own[2].wait()
    for copy in got_q:
        copy.wait_recv()
    for h in range(HEADS):
        cols = slice(h * HEAD_DIM, (h + 1) * HEAD_DIM)
        qh[:, cols] = load_rows(qb, cols)
    image_chunk(0)

    for copy in got_rep:
        copy.wait_recv()
    got_txt = [send(txt.at[0], txt.at[d], S_TX + d, x_peer(d)) for d in range(1, NX)]

    v_right.wait_recv()
    image_chunk(1)
    k_left.wait_recv()
    image_chunk(3)
    k_far.wait_recv()
    v_far.wait_recv()
    image_chunk(2)
    for copy in got_txt:
        copy.wait_recv()

    flags = txt[:, :, :, 2 * WIDE : PACKED].reshape(NX * TEXT, 128)
    ones = jnp.ones((16, 128), bf16)
    live = lax.dot_general(ones, flags, (((1,), (1,)), ((), ())), preferred_element_type=f32)[0:1] > 0.5

    def text_chunk(h, carry):
        at_k = pl.ds(pl.multiple_of(h * HEAD_DIM, HEAD_DIM), HEAD_DIM)
        at_v = pl.ds(pl.multiple_of((h + HEADS) * HEAD_DIM, HEAD_DIM), HEAD_DIM)
        keys = txt[:, :, :, at_k].reshape(NX * TEXT, HEAD_DIM)
        values = txt[:, :, :, at_v].reshape(NX * TEXT, HEAD_DIM)
        update(h, keys, values, live)
        return carry

    lax.fori_loop(0, HEADS, text_chunk, 0)

    for h in range(HEADS):
        result = (o[h] / l[h]).reshape(GROUPS, IMG_DEV, HEAD_DIM)
        o_s[:, :, h * HEAD_DIM : (h + 1) * HEAD_DIM] = result.astype(bf16)
    for d in range(1, GROUPS):
        send(o_s.at[d], out.at[0, :, columns(gi)], S_OUT + d, group_peer(GROUPS - d))
    last = pltpu.make_async_copy(o_s.at[0], out.at[0, :, columns(gi)], lsem.at[5])
    last.start()
    for d in range(1, GROUPS):
        there = columns(lax.rem(gi + d, GROUPS))
        remote(o_s.at[d], out.at[0, :, there], S_OUT + d, group_peer(d)).wait_recv()
    last.wait()
    for copy in sent:
        copy.wait_send()


def local(text_rows, modulation, timestep, row_request, w_key, w_value, q_image, k_image, v_image):
    f32, bf16 = jnp.float32, jnp.bfloat16
    vmem = pl.BlockSpec(memory_space=pltpu.VMEM)
    smem = pl.BlockSpec(memory_space=pltpu.SMEM)
    hbm = pl.BlockSpec(memory_space=pl.ANY)
    features = text_rows.shape[1]
    return pl.pallas_call(
        kernel,
        out_shape=jax.ShapeDtypeStruct(q_image.shape, bf16),
        in_specs=[vmem, vmem, smem, vmem, hbm, hbm, hbm, hbm, hbm],
        out_specs=hbm,
        scratch_shapes=[
            pltpu.VMEM((NY, ROWS, features), bf16),
            pltpu.VMEM((NY, 2 * REPS, features), f32),
            pltpu.VMEM((NY, features, WIDE), bf16),
            pltpu.VMEM((NY, features, WIDE), bf16),
            pltpu.VMEM((GROUPS, IMG_DEV, WIDE), bf16),
            pltpu.VMEM((NX, 2, GROUPS, IMG_DEV, WIDE), bf16),
            pltpu.VMEM((8, ROWS), f32),
            pltpu.VMEM((NX, 8, ROWS), f32),
            pltpu.VMEM((ROWS, 2 * WIDE), f32),
            pltpu.VMEM((ROWS, 2 * WIDE), bf16),
            pltpu.VMEM((NX, QUARTER, 2 * WIDE), bf16),
            pltpu.VMEM((REPS, SLOTS, PACKED), bf16),
            pltpu.VMEM((NX, REPS, SLOTS, PACKED), bf16),
            pltpu.VMEM((CHUNK, WIDE), bf16),
            pltpu.VMEM((HEADS, CHUNK, HEAD_DIM), f32),
            pltpu.VMEM((HEADS, CHUNK, HEAD_DIM), f32),
            pltpu.VMEM((HEADS, CHUNK, HEAD_DIM), f32),
            pltpu.VMEM((GROUPS, IMG_DEV, WIDE), bf16),
            pltpu.SemaphoreType.DMA((S_ALL,)),
            pltpu.SemaphoreType.DMA((S_ALL,)),
            pltpu.SemaphoreType.DMA((6,)),
        ],
        compiler_params=pltpu.CompilerParams(
            collective_id=0, has_side_effects=True, vmem_limit_bytes=40 * 1024 * 1024
        ),
    )(text_rows, modulation, timestep, row_request, w_key, w_value, q_image, k_image, v_image)


def solution(mesh):
    image = P("rep", ("seq", "chip"), None)
    return jax.shard_map(
        local,
        mesh=mesh,
        in_specs=(
            P("rep", "seq"),
            P(None, None, "seq"),
            P(),
            P("rep", None),
            P("seq", "chip"),
            P("seq", "chip"),
            image,
            image,
            image,
        ),
        out_specs=image,
        check_vma=False,
    )
```

time: 879 us -> 87.8 us (0.10)
  waiting for transfers between devices: 703 us -> 0 us
  Pallas kernels: 0 us -> 79.9 us
  blocking collectives: 73.6 us -> 0 us
  local copies, waits for them, and re-layouts: 46.7 us -> 7.56 us
  matrix products: 27 us -> 0 us
  between operations: 14.4 us -> 0.06 us
  starting transfers between devices: 8.86 us -> 0 us
    all_gather x6 -> x0, waiting for transfers between devices: 614 us -> none  [the longest x1 241 us: local(): lax.all_gather(k_image[0], ('seq', 'chip'), axis=0, tiled=True)]
    reduce_scatter x1 -> x0, waiting for transfers between devices: 81.9 us -> none  [local(): lax.psum_scatter(jnp.dot(shaped, w_both, preferred_element_type=jnp.float...]
    pallas_call x0 -> x1, Pallas kernels: none -> 79.9 us  [local(): pl.pallas_call(kernel, out_shape=jax.ShapeDtypeStruct(q_image.shape, bf16...]
    all_gather x4 -> x0, local copies, waits for them, and re-layouts: 35.7 us -> none  [the longest x1 14 us: local(): lax.all_gather(v_image[0], ('seq', 'chip'), axis=0, tiled=True)]
    psum x1 -> x0, blocking collectives: 34.3 us -> none  [local(): lax.psum((jnp.sum(values_text, axis=1), jnp.sum(values_text * values_text...]
    all_to_all x2 -> x0, blocking collectives: 28 us -> none  [the longest x1 16.7 us: local(): lax.all_to_all(send_keys, 'rep', split_axis=0, concat_axis=0, tiled=True)]
    dot_general x9 -> x0, matrix products: 27 us -> none  [the longest x2 14.3 us: block_update(): jnp.einsum('hqk,khd->hqd', weights.astype(jnp.bfloat16), valued, preferre...]
    unnamed x1 -> x0, blocking collectives: 11.3 us -> none
  transfers between devices with their start and end apart: 8 -> 0, of which waited for: 8 -> 0; matrix products, arithmetic and copies ran while one was open for 4% -> 0% of each run, Pallas kernels for 0% -> 0%
where the time goes in v1:
time: 87.8 us; the launch traced here: 87.5 us
  Pallas kernels  79.9 us (91%)
  local copies, waits for them, and re-layouts  7.56 us (9%)
    pallas_call x1, Pallas kernels, local(): pl.pallas_call(kernel, out_shape=jax.ShapeDtypeStruct(q_image.shape, bf16...  79.9 us
    unnamed x17, local copies, waits for them, and re-layouts  7.56 us

profile of v1, /device:TPU:1, one launch (start us, length us, event | category | flops | bytes accessed | tf_op | source)
XLA Modules:
  0.0 87.5 jit_solution(14878980935401258462)
XLA Ops:
  0.0 0.0 copy-start.2
  0.0 1.0 %copy.10.text = bf16[256,192]{1,0:T(8,128)(2,1)S(1)} copy(bf16[256,192]{0,1:T(8,128)(2,1)} %param.9) | data formatting | bytes 196608 | tf_op args[0]
  1.0 0.0 copy-start.6
  1.1 0.8 copy.11.req
  1.9 0.0 copy-done.2
  1.9 0.0 copy-done.6
  1.9 0.0 copy-start
  1.9 1.1 %copy-done = bf16[192,1536]{1,0:T(8,128)(2,1)S(1)} copy-done((bf16[192,1536]{1,0:T(8,128)(2,1)S(1)}, bf16[192,1536]{1,0:T(8,128)(2,1)}, u32[]{:S(2)}) %copy-start) | copy-done | bytes 589848
  3.0 0.0 copy-start.1
  3.0 1.1 %copy-done.1 = bf16[192,1536]{1,0:T(8,128)(2,1)S(1)} copy-done((bf16[192,1536]{1,0:T(8,128)(2,1)S(1)}, bf16[192,1536]{1,0:T(8,128)(2,1)}, u32[]{:S(2)}) %copy-start.1) | copy-done | bytes 589848
  4.0 0.0 copy-start.3
  4.0 1.0 %copy-done.3 = bf16[1,56,3072]{2,1,0:T(8,128)(2,1)S(1)} copy-done((bf16[1,56,3072]{2,1,0:T(8,128)(2,1)S(1)}, bf16[1,56,3072]{2,1,0:T(8,128)(2,1)}, u32[]{:S(2)}) %copy-start.3) | copy-done | bytes 344088
  5.0 0.0 copy-start.4
  5.0 1.0 %copy-done.4 = bf16[1,56,3072]{2,1,0:T(8,128)(2,1)S(1)} copy-done((bf16[1,56,3072]{2,1,0:T(8,128)(2,1)S(1)}, bf16[1,56,3072]{2,1,0:T(8,128)(2,1)}, u32[]{:S(2)}) %copy-start.4) | copy-done | bytes 344088
  6.0 0.0 copy-start.5
  6.0 0.9 %copy-done.5 = f32[50,2,192]{2,1,0:T(2,128)S(1)} copy-done((f32[50,2,192]{2,1,0:T(2,128)S(1)}, f32[50,2,192]{2,1,0:T(2,128)}, u32[]{:S(2)}) %copy-start.5) | copy-done | bytes 76824
  6.9 79.9 %shard_map.91 = bf16[1,56,3072]{2,1,0:T(8,128)(2,1)S(1)} custom-call(bf16[256,192]{1,0:T(8,128)(2,1)S(1)} %copy.10.text, f32[50,2,192]{2,1,0:T(2,128)S(1)} %copy-done.5, s32[8]{0:T(128)S(1)} %copy-done.6, s32[256,1]{1,0:T(8,128)S(1)} %copy.11.req, bf16[192,1536]{1,0:T(8,128)(2,1)S(1)} %copy-done, bf16[192,1536]{1,0:T(8,128)(2,1)S(1)} %copy-done.1, ...), custom_call_target="tpu_custom_call" | custom-call | tf_op jit(solution)/shard_map/pallas_call | solution.py:300
  86.8 0.7 copy.13
Async XLA Ops:
  0.0 1.9 %copy-start.2 = (bf16[1,56,3072]{2,1,0:T(8,128)(2,1)S(1)}, bf16[1,56,3072]{2,1,0:T(8,128)(2,1)}, u32[]{:S(2)}) copy-start(bf16[1,56,3072]{2,1,0:T(8,128)(2,1)} %q_in.1) | copy-start | bytes 1032196
  1.0 0.8 copy-start.6
  1.9 1.1 %copy-start = (bf16[192,1536]{1,0:T(8,128)(2,1)S(1)}, bf16[192,1536]{1,0:T(8,128)(2,1)}, u32[]{:S(2)}) copy-start(bf16[192,1536]{1,0:T(8,128)(2,1)} %w_key.1) | copy-start | bytes 1769476
  3.0 1.1 %copy-start.1 = (bf16[192,1536]{1,0:T(8,128)(2,1)S(1)}, bf16[192,1536]{1,0:T(8,128)(2,1)}, u32[]{:S(2)}) copy-start(bf16[192,1536]{1,0:T(8,128)(2,1)} %w_value.1) | copy-start | bytes 1769476
  4.0 1.0 %copy-start.3 = (bf16[1,56,3072]{2,1,0:T(8,128)(2,1)S(1)}, bf16[1,56,3072]{2,1,0:T(8,128)(2,1)}, u32[]{:S(2)}) copy-start(bf16[1,56,3072]{2,1,0:T(8,128)(2,1)} %k_in.1) | copy-start | bytes 1032196
  5.0 1.0 %copy-start.4 = (bf16[1,56,3072]{2,1,0:T(8,128)(2,1)S(1)}, bf16[1,56,3072]{2,1,0:T(8,128)(2,1)}, u32[]{:S(2)}) copy-start(bf16[1,56,3072]{2,1,0:T(8,128)(2,1)} %v_in.1) | copy-start | bytes 1032196
  6.0 0.9 %copy-start.5 = (f32[50,2,192]{2,1,0:T(2,128)S(1)}, f32[50,2,192]{2,1,0:T(2,128)}, u32[]{:S(2)}) copy-start(f32[50,2,192]{2,1,0:T(2,128)} %mod.1) | copy-start | bytes 230404

commit v2 on v0

v2 whole, which is shorter than its diff:
```python
import math

import jax
import jax.numpy as jnp
from jax import lax
from jax.experimental import pallas as pl
from jax.experimental.pallas import tpu as pltpu
from jax.sharding import PartitionSpec as P

D = 3072
HEAD_DIM = 128
CAP = 4
BLOCK = 16
NX = 4
NY = 4
NZ = 2
REPS = 8
PLANE = NX * NY
GROUP = PLANE * NZ
ROLES = 3
WIDE = ROLES * HEAD_DIM
IMG_DEV = 56
IMG = GROUP * IMG_DEV
SLOTS_PER_STEP = 8
STEP = SLOTS_PER_STEP * IMG_DEV
STEPS = GROUP // SLOTS_PER_STEP
ROWS = 256
SLOTS = ROWS // BLOCK * CAP
TEXT = REPS * SLOTS
HALF = 96
FACTOR = math.log2(math.e) / math.sqrt(HEAD_DIM)
LOWEST = -1e30
VMEM_LIMIT = 60 * 1024 * 1024
MESH = pl.DeviceIdType.MESH

S_TEXT, S_MOD, S_STAT, S_REQ = 0, 1, 2, 3
S_W, S_WC, S_SUM, S_REP = 4, 6, 8, 10
S_K, S_Q, S_V, S_OUT = 12, 13, 14, 15
S_ALL = 16


def kernel(
    text, mod, step, req, w_key, w_value, q_in, k_in, v_in, out,
    tx, mod_v, md, rq, w, qb, kb, vb, stats, xs, acc, sum_s, sum_r,
    place_t, rep_s, landed, qh, kh, vh, m, l, o, o_s,
    ssem, rsem, lsem,
):
    f32, bf16 = jnp.float32, jnp.bfloat16
    rep, seq, z = lax.axis_index("rep"), lax.axis_index("seq"), lax.axis_index("chip")
    y, x = lax.div(seq, NX), lax.rem(seq, NX)
    role = lax.rem(x + y, NX)
    active = role < ROLES
    idle = role >= ROLES

    def group_at(px, py, pz):
        return (rep, py * NX + px, pz)

    def ahead(i):
        px = lax.rem(x + lax.rem(i, NX), NX)
        py = lax.rem(y + lax.rem(lax.div(i, NX), NY), NY)
        pz = lax.rem(z + lax.div(i, PLANE), NZ)
        return px, py, pz

    def behind(i):
        px = lax.rem(x + NX - lax.rem(i, NX), NX)
        py = lax.rem(y + NY - lax.rem(lax.div(i, NX), NY), NY)
        pz = lax.rem(z + NZ - lax.div(i, PLANE), NZ)
        return px, py, pz

    def x_peer(d):
        return (rep, y * NX + lax.rem(x + d, NX), z)

    def y_peer(d):
        return (rep, lax.rem(y + d, NY) * NX + x, z)

    def rep_peer(d):
        return (lax.rem(rep + d, REPS), seq, z)

    def head_columns(head):
        return pl.ds(pl.multiple_of(head * HEAD_DIM, HEAD_DIM), HEAD_DIM)

    def columns(index):
        return pl.ds(pl.multiple_of(index * WIDE, WIDE), WIDE)

    own_head = head_columns((z * NY + y) * ROLES + role)

    def remote(src, dst, index, peer):
        return pltpu.make_async_remote_copy(
            src_ref=src, dst_ref=dst, send_sem=ssem.at[index], recv_sem=rsem.at[index],
            device_id=peer, device_id_type=MESH,
        )

    def send(src, dst, index, peer):
        remote(src, dst, index, peer).start()

    def arrived(ref, index):
        remote(ref, ref, index, x_peer(1)).wait_recv()

    def left(ref, index):
        remote(ref, ref, index, x_peer(1)).wait_send()

    barrier = pltpu.get_barrier_semaphore()

    def greet(i, carry):
        pl.semaphore_signal(barrier, inc=1, device_id=group_at(*ahead(i)), device_id_type=MESH)
        return carry

    lax.fori_loop(1, GROUP, greet, 0)
    for d in range(1, REPS):
        pl.semaphore_signal(barrier, inc=1, device_id=rep_peer(d), device_id_type=MESH)

    own = [
        pltpu.make_async_copy(text, tx.at[0], lsem.at[0]),
        pltpu.make_async_copy(mod, mod_v, lsem.at[1]),
        pltpu.make_async_copy(req, rq.at[0], lsem.at[2]),
        pltpu.make_async_copy(w_key.at[:, columns(y)], w.at[0, 0], lsem.at[3]),
        pltpu.make_async_copy(w_value.at[:, columns(y)], w.at[1, 0], lsem.at[4]),
    ]
    own_text, own_mod, own_req, own_wk, own_wv = own
    for copy in own:
        copy.start()
    own_image = [(k_in, kb, 5), (q_in, qb, 6), (v_in, vb, 7)]

    @pl.when(active)
    def _():
        for src, dst, index in own_image:
            pltpu.make_async_copy(src.at[0, :, own_head], dst.at[0], lsem.at[index]).start()

    pl.semaphore_wait(barrier, GROUP - 1 + REPS - 1)

    for d in range(1, NY):
        send(text, tx.at[d], S_TEXT, y_peer(d))

    own_mod.wait()
    for g in range(REPS):
        md[0, 2 * g : 2 * g + 2, :] = mod_v[step[g]]
    for d in range(1, NY):
        send(md.at[0], md.at[d], S_MOD, y_peer(d))

    own_text.wait()
    part = tx[0].astype(f32)
    stats[0] = jnp.concatenate(
        [
            jnp.sum(part, axis=0, keepdims=True),
            jnp.sum(part * part, axis=0, keepdims=True),
            jnp.zeros((6, ROWS), f32),
        ],
        axis=0,
    )

    def send_stats(i, carry):
        send(stats.at[0], stats.at[i], S_STAT, group_at(*ahead(i)))
        return carry

    lax.fori_loop(1, PLANE, send_stats, 0)

    core = lax.rem(rep, 2)
    sibling = (rep + 1 - 2 * core, seq, z)
    half = pl.ds(pl.multiple_of(core * HALF, HALF), HALF)
    for part, src in ((0, w_key), (1, w_value)):
        for d in range(1, NY):
            there = columns(lax.rem(y + d, NY))
            send(src.at[half, there], w.at[part, d, half], S_W + part, y_peer(d))

    def send_image(i, carry):
        px, py, pz = ahead(i)
        its_role = lax.rem(px + py, NX)

        @pl.when(its_role < ROLES)
        def _():
            there = head_columns((pz * NY + py) * ROLES + its_role)
            peer = group_at(px, py, pz)
            send(k_in.at[0, :, there], kb.at[i], S_K, peer)
            send(q_in.at[0, :, there], qb.at[i], S_Q, peer)
            send(v_in.at[0, :, there], vb.at[i], S_V, peer)

        return carry

    lax.fori_loop(1, GROUP, send_image, 0)
    for d in range(1, REPS):
        send(req, rq.at[d], S_REQ, rep_peer(d))

    own_req.wait()
    request = rq[0]
    sub16 = lax.broadcasted_iota(jnp.int32, (16, ROWS), 0)
    is_target = sub16 == request
    first_row = lax.broadcasted_iota(jnp.int32, (ROWS, ROWS), 0)
    second_row = lax.broadcasted_iota(jnp.int32, (ROWS, ROWS), 1)
    earlier = (first_row < second_row).astype(f32).astype(bf16)
    count = jnp.dot(is_target.astype(f32).astype(bf16), earlier, preferred_element_type=f32)
    slot = jnp.sum(jnp.where(is_target, count, 0.0), axis=0, keepdims=True).astype(jnp.int32)
    is_place = lax.broadcasted_iota(jnp.int32, (TEXT, ROWS), 0) == request * SLOTS + slot
    place_t[...] = is_place.astype(f32).astype(bf16)
    pick_shift = (sub16 == 2 * request).astype(f32)
    pick_scale = (sub16 == 2 * request + 1).astype(f32)

    arrived(md.at[1:NY], S_MOD)
    arrived(stats.at[1:PLANE], S_STAT)
    summed = stats[0]
    for i in range(1, PLANE):
        summed = summed + stats[i]
    mean = summed[0:1] / D
    power = summed[1:2] / D
    scaled = lax.rsqrt(power - mean * mean + 1e-06)
    over_rows = (((0,), (0,)), ((), ()))
    arrived(tx.at[1:NY], S_TEXT)
    for d in range(NY):
        shift = lax.dot_general(
            md[d], pick_shift, over_rows, precision=lax.Precision.HIGHEST, preferred_element_type=f32
        )
        scale = lax.dot_general(
            md[d], pick_scale, over_rows, precision=lax.Precision.HIGHEST, preferred_element_type=f32
        )
        shaped = (tx[d].astype(f32) - mean) * scaled * (1.0 + scale) + shift
        xs[d] = shaped.astype(bf16)

    for part in range(2):
        arrived(w.at[part, 1:NY, half], S_W + part)
        send(w.at[part, 1:NY, half], w.at[part, 1:NY, half], S_WC + part, sibling)

    for part, copy in ((0, own_wk), (1, own_wv)):
        copy.wait()
        arrived(w.at[part, 1:NY, half], S_WC + part)
        acc[part] = lax.dot_general(
            xs[...].reshape(D // NX, ROWS), w[part].reshape(D // NX, WIDE), over_rows,
            preferred_element_type=f32,
        )
        sum_s[part] = acc[part].astype(bf16)
        for d in range(1, NX):
            its_role = lax.rem(x + d + y, NX)

            @pl.when(its_role < ROLES)
            def _(part=part, d=d, its_role=its_role):
                src = sum_s.at[part, :, head_columns(its_role)]
                send(src, sum_r.at[part, d], S_SUM + part, x_peer(d))

    @pl.when(active)
    def _():
        for part in range(2):
            arrived(sum_r.at[part, 1:NX], S_SUM + part)
            rows = acc[part, :, head_columns(role)]
            for d in range(1, NX):
                rows = rows + sum_r[part, d].astype(f32)
            moved = jnp.dot(place_t[...], rows.astype(bf16), preferred_element_type=f32)
            rep_s[part] = moved.astype(bf16).reshape(REPS, SLOTS, HEAD_DIM)
            for d in range(1, REPS):
                src = rep_s.at[part, lax.rem(rep + d, REPS)]
                send(src, landed.at[part, d], S_REP + part, rep_peer(d))
            landed[part, 0] = rep_s[part, rep]

        for (src, dst, index), index_all in zip(own_image, (S_K, S_Q, S_V)):
            pltpu.make_async_copy(src.at[0, :, own_head], dst.at[0], lsem.at[index]).wait()
            arrived(dst.at[1:GROUP], index_all)

        def flatten(b, carry):
            slots = pl.ds(b * SLOTS_PER_STEP, SLOTS_PER_STEP)
            rows = pl.ds(pl.multiple_of(b * STEP, STEP), STEP)
            for src, dst in ((kb, kh), (qb, qh), (vb, vh)):
                dst[rows, :] = src[slots].astype(f32).reshape(STEP, HEAD_DIM).astype(bf16)
            return carry

        lax.fori_loop(0, STEPS, flatten, 0)

        over_columns = (((1,), (1,)), ((), ()))

        def image_step(b, carry):
            rows = pl.ds(pl.multiple_of(b * STEP, STEP), STEP)
            s = lax.dot_general(qh[rows, :], kh[...], over_columns, preferred_element_type=f32)
            highest = jnp.max(s, axis=1, keepdims=True)
            weights = jnp.exp2((s - highest) * FACTOR)
            m[rows, :] = jnp.broadcast_to(highest, (STEP, HEAD_DIM))
            l[rows, :] = jnp.broadcast_to(jnp.sum(weights, axis=1, keepdims=True), (STEP, HEAD_DIM))
            o[rows, :] = jnp.dot(weights.astype(bf16), vh[...], preferred_element_type=f32)
            return carry

        lax.fori_loop(0, STEPS, image_step, 0)

        arrived(rq.at[1:REPS], S_REQ)
        named = jnp.concatenate([rq[d] for d in range(REPS)], axis=0) == rep
        counted = jnp.sum(jnp.where(named, 1.0, 0.0), axis=1, keepdims=True)
        lane = lax.broadcasted_iota(jnp.int32, (REPS, TEXT), 1)
        in_rep = lax.broadcasted_iota(jnp.int32, (REPS, TEXT), 0) == lax.div(lane, SLOTS)
        bound = jnp.sum(jnp.where(in_rep, counted, 0.0), axis=0, keepdims=True)
        live = lax.rem(lane, SLOTS)[0:1].astype(f32) < bound

        for part in range(2):
            arrived(landed.at[part, 1:REPS], S_REP + part)

        def text_step(b, carry):
            rows = pl.ds(pl.multiple_of(b * STEP, STEP), STEP)
            keys = landed[0].reshape(TEXT, HEAD_DIM)
            values = landed[1].reshape(TEXT, HEAD_DIM)
            s = lax.dot_general(qh[rows, :], keys, over_columns, preferred_element_type=f32)
            s = jnp.where(live, s, LOWEST)
            before = m[rows, :]
            newest = jnp.maximum(before, jnp.max(s, axis=1, keepdims=True))
            weights = jnp.exp2((s - newest[:, 0:1]) * FACTOR)
            fade = jnp.exp2((before - newest) * FACTOR)
            total = l[rows, :] * fade + jnp.sum(weights, axis=1, keepdims=True)
            mixed = o[rows, :] * fade + jnp.dot(weights.astype(bf16), values, preferred_element_type=f32)
            result = (mixed / total).reshape(SLOTS_PER_STEP, IMG_DEV, HEAD_DIM)
            o_s[pl.ds(b * SLOTS_PER_STEP, SLOTS_PER_STEP)] = result.astype(bf16)

            def send_result(k, inner):
                i = b * SLOTS_PER_STEP + k

                @pl.when(i > 0)
                def _():
                    send(o_s.at[i], out.at[0, :, own_head], S_OUT, group_at(*behind(i)))

                return inner

            lax.fori_loop(0, SLOTS_PER_STEP, send_result, 0)
            return carry

        lax.fori_loop(0, STEPS, text_step, 0)
        last = pltpu.make_async_copy(o_s.at[0], out.at[0, :, own_head], lsem.at[8])
        last.start()
        arrived(out.at[0, :, 0 : (NY * NZ * ROLES - 1) * HEAD_DIM], S_OUT)
        last.wait()
        left(o_s.at[1:GROUP], S_OUT)
        for index in (S_K, S_Q, S_V):
            left(kb.at[1 : NY * NZ * ROLES], index)
        for part in range(2):
            left(sum_r.at[part, 1 : NX - 1], S_SUM + part)
            left(landed.at[part, 1:REPS], S_REP + part)

    @pl.when(idle)
    def _():
        arrived(rq.at[1:REPS], S_REQ)
        arrived(out.at[0], S_OUT)
        for index in (S_K, S_Q, S_V):
            left(kb.at[0 : NY * NZ * ROLES], index)
        for part in range(2):
            left(sum_r.at[part, 1:NX], S_SUM + part)

    left(tx.at[1:NY], S_TEXT)
    left(md.at[1:NY], S_MOD)
    left(stats.at[1:PLANE], S_STAT)
    left(rq.at[1:REPS], S_REQ)
    for part in range(2):
        left(w.at[part, 1:NY, half], S_W + part)
        left(w.at[part, 1:NY, half], S_WC + part)


def local(text_rows, modulation, timestep, row_request, w_key, w_value, q_image, k_image, v_image):
    f32, bf16 = jnp.float32, jnp.bfloat16
    smem = pl.BlockSpec(memory_space=pltpu.SMEM)
    hbm = pl.BlockSpec(memory_space=pl.ANY)
    features = text_rows.shape[1]
    blocks = pltpu.VMEM((GROUP, IMG_DEV, HEAD_DIM), bf16)
    return pl.pallas_call(
        kernel,
        out_shape=jax.ShapeDtypeStruct(q_image.shape, bf16),
        in_specs=[hbm, hbm, smem, hbm, hbm, hbm, hbm, hbm, hbm],
        out_specs=hbm,
        scratch_shapes=[
            pltpu.VMEM((NY, features, ROWS), bf16),
            pltpu.VMEM(modulation.shape, f32),
            pltpu.VMEM((NY, 2 * REPS, features), f32),
            pltpu.VMEM((REPS, 1, ROWS), jnp.int32),
            pltpu.VMEM((2, NY, features, WIDE), bf16),
            blocks,
            blocks,
            blocks,
            pltpu.VMEM((PLANE, 8, ROWS), f32),
            pltpu.VMEM((NY, features, ROWS), bf16),
            pltpu.VMEM((2, ROWS, WIDE), f32),
            pltpu.VMEM((2, ROWS, WIDE), bf16),
            pltpu.VMEM((2, NX, ROWS, HEAD_DIM), bf16),
            pltpu.VMEM((TEXT, ROWS), bf16),
            pltpu.VMEM((2, REPS, SLOTS, HEAD_DIM), bf16),
            pltpu.VMEM((2, REPS, SLOTS, HEAD_DIM), bf16),
            pltpu.VMEM((IMG, HEAD_DIM), bf16),
            pltpu.VMEM((IMG, HEAD_DIM), bf16),
            pltpu.VMEM((IMG, HEAD_DIM), bf16),
            pltpu.VMEM((IMG, HEAD_DIM), f32),
            pltpu.VMEM((IMG, HEAD_DIM), f32),
            pltpu.VMEM((IMG, HEAD_DIM), f32),
            blocks,
            pltpu.SemaphoreType.DMA((S_ALL,)),
            pltpu.SemaphoreType.DMA((S_ALL,)),
            pltpu.SemaphoreType.DMA((9,)),
        ],
        compiler_params=pltpu.CompilerParams(
            collective_id=0, has_side_effects=True, vmem_limit_bytes=VMEM_LIMIT
        ),
    )(
        text_rows.T, modulation, timestep, row_request.reshape(1, -1),
        w_key, w_value, q_image, k_image, v_image,
    )


def solution(mesh):
    image = P("rep", ("seq", "chip"), None)
    return jax.shard_map(
        local,
        mesh=mesh,
        in_specs=(
            P("rep", "seq"),
            P(None, None, "seq"),
            P(),
            P("rep", None),
            P("seq", "chip"),
            P("seq", "chip"),
            image,
            image,
            image,
        ),
        out_specs=image,
        check_vma=False,
    )
```

time: 879 us -> 70 us (0.08)
  waiting for transfers between devices: 703 us -> 0 us
  blocking collectives: 73.6 us -> 0 us
  Pallas kernels: 0 us -> 68.1 us
  local copies, waits for them, and re-layouts: 46.7 us -> 1.73 us
  matrix products: 27 us -> 0 us
  between operations: 14.4 us -> 0.01 us
  starting transfers between devices: 8.86 us -> 0 us
    all_gather x6 -> x0, waiting for transfers between devices: 614 us -> none  [the longest x1 241 us: local(): lax.all_gather(k_image[0], ('seq', 'chip'), axis=0, tiled=True)]
    reduce_scatter x1 -> x0, waiting for transfers between devices: 81.9 us -> none  [local(): lax.psum_scatter(jnp.dot(shaped, w_both, preferred_element_type=jnp.float...]
    pallas_call x0 -> x1, Pallas kernels: none -> 68.1 us  [local(): pl.pallas_call(kernel, out_shape=jax.ShapeDtypeStruct(q_image.shape, bf16...]
    all_gather x4 -> x0, local copies, waits for them, and re-layouts: 35.7 us -> none  [the longest x1 14 us: local(): lax.all_gather(v_image[0], ('seq', 'chip'), axis=0, tiled=True)]
    psum x1 -> x0, blocking collectives: 34.3 us -> none  [local(): lax.psum((jnp.sum(values_text, axis=1), jnp.sum(values_text * values_text...]
    all_to_all x2 -> x0, blocking collectives: 28 us -> none  [the longest x1 16.7 us: local(): lax.all_to_all(send_keys, 'rep', split_axis=0, concat_axis=0, tiled=True)]
    dot_general x9 -> x0, matrix products: 27 us -> none  [the longest x2 14.3 us: block_update(): jnp.einsum('hqk,khd->hqd', weights.astype(jnp.bfloat16), valued, preferre...]
    unnamed x1 -> x0, blocking collectives: 11.3 us -> none
  transfers between devices with their start and end apart: 8 -> 0, of which waited for: 8 -> 0; matrix products, arithmetic and copies ran while one was open for 4% -> 0% of each run, Pallas kernels for 0% -> 0%
where the time goes in v2:
time: 70 us; the launch traced here: 69.9 us
  Pallas kernels  68.1 us (97%)
  local copies, waits for them, and re-layouts  1.73 us (2%)
    pallas_call x1, Pallas kernels, local(): pl.pallas_call(kernel, out_shape=jax.ShapeDtypeStruct(q_image.shape, bf16...  68.1 us
    unnamed x1, local copies, waits for them, and re-layouts  1.73 us

profile of v2, /device:TPU:1, one launch (start us, length us, event | category | flops | bytes accessed | tf_op | source)
XLA Modules:
  0.0 69.9 jit_solution(14296205280074211323)
XLA Ops:
  0.0 68.1 %shard_map.91 = bf16[1,56,3072]{2,1,0:T(8,128)(2,1)} custom-call(bf16[192,256]{1,0:T(8,128)(2,1)} %bitcast.2, f32[50,2,192]{2,1,0:T(2,128)} %mod.1, s32[8]{0:T(128)} %step.1, s32[1,256]{1,0:T(1,128)} %bitcast.3, bf16[192,1536]{1,0:T(8,128)(2,1)} %w_key.1, bf16[192,1536]{1,0:T(8,128)(2,1)} %w_value.1, bf16[1,56,3072]{2,1,0:T(8,128)(2,1)} %q_in.1, ...), custom_call_target="tpu_custom_call" | custom-call | tf_op jit(solution)/shard_map/pallas_call | solution.py:352
  68.1 1.7 %copy.11 = bf16[1,56,3072]{2,1,0:T(8,128)(2,1)} copy(bf16[1,56,3072]{2,1,0:T(8,128)(2,1)} %shard_map.91) | data formatting | bytes 688128

commit v3 on v2

--- a/solution.py
+++ b/solution.py
@@ -35,13 +35,13 @@
 
 S_TEXT, S_MOD, S_STAT, S_REQ = 0, 1, 2, 3
 S_W, S_WC, S_SUM, S_REP = 4, 6, 8, 10
-S_K, S_Q, S_V, S_OUT = 12, 13, 14, 15
-S_ALL = 16
+S_OUT, S_HOP, S_LAST = 12, 13, 16
+S_ALL = 28
 
 
 def kernel(
     text, mod, step, req, w_key, w_value, q_in, k_in, v_in, out,
-    tx, mod_v, md, rq, w, qb, kb, vb, stats, xs, acc, sum_s, sum_r,
+    tx, mod_v, md, rq, w, relay, final, stats, xs, acc, sum_s, sum_r,
     place_t, rep_s, landed, qh, kh, vh, m, l, o, o_s,
     ssem, rsem, lsem,
 ):
@@ -55,17 +55,16 @@
     def group_at(px, py, pz):
         return (rep, py * NX + px, pz)
 
+    def offsets(i):
+        return lax.rem(i, NX), lax.div(i, SLOTS_PER_STEP), lax.rem(lax.div(i, NX), NZ)
+
     def ahead(i):
-        px = lax.rem(x + lax.rem(i, NX), NX)
-        py = lax.rem(y + lax.rem(lax.div(i, NX), NY), NY)
-        pz = lax.rem(z + lax.div(i, PLANE), NZ)
-        return px, py, pz
+        dx, dy, dz = offsets(i)
+        return lax.rem(x + dx, NX), lax.rem(y + dy, NY), lax.rem(z + dz, NZ)
 
     def behind(i):
-        px = lax.rem(x + NX - lax.rem(i, NX), NX)
-        py = lax.rem(y + NY - lax.rem(lax.div(i, NX), NY), NY)
-        pz = lax.rem(z + NZ - lax.div(i, PLANE), NZ)
-        return px, py, pz
+        dx, dy, dz = offsets(i)
+        return lax.rem(x + NX - dx, NX), lax.rem(y + NY - dy, NY), lax.rem(z + NZ - dz, NZ)
 
     def x_peer(d):
         return (rep, y * NX + lax.rem(x + d, NX), z)
@@ -119,12 +118,26 @@
     own_text, own_mod, own_req, own_wk, own_wv = own
     for copy in own:
         copy.start()
-    own_image = [(k_in, kb, 5), (q_in, qb, 6), (v_in, vb, 7)]
-
-    @pl.when(active)
-    def _():
-        for src, dst, index in own_image:
-            pltpu.make_async_copy(src.at[0, :, own_head], dst.at[0], lsem.at[index]).start()
+    def role_at(px, py):
+        return lax.rem(px + py, NX)
+
+    def head_at(px, py, pz):
+        return head_columns((pz * NY + py) * ROLES + role_at(px, py))
+
+    image = (q_in, k_in, v_in)
+
+    def own_hop(t, d):
+        py = lax.rem(y + d, NY)
+        return pltpu.make_async_copy(
+            image[t].at[0, :, head_at(x, py, z)], relay.at[t, d, 0], lsem.at[5 + NY * t + d]
+        )
+
+    for d in range(NY):
+
+        @pl.when(role_at(x, y + d) < ROLES)
+        def _(d=d):
+            for t in range(3):
+                own_hop(t, d).start()
 
     pl.semaphore_wait(barrier, GROUP - 1 + REPS - 1)
 
@@ -149,7 +162,8 @@
     )
 
     def send_stats(i, carry):
-        send(stats.at[0], stats.at[i], S_STAT, group_at(*ahead(i)))
+        px, py = lax.rem(x + lax.rem(i, NX), NX), lax.rem(y + lax.div(i, NX), NY)
+        send(stats.at[0], stats.at[i], S_STAT, group_at(px, py, z))
         return carry
 
     lax.fori_loop(1, PLANE, send_stats, 0)
@@ -162,21 +176,21 @@
             there = columns(lax.rem(y + d, NY))
             send(src.at[half, there], w.at[part, d, half], S_W + part, y_peer(d))
 
-    def send_image(i, carry):
-        px, py, pz = ahead(i)
-        its_role = lax.rem(px + py, NX)
-
-        @pl.when(its_role < ROLES)
-        def _():
-            there = head_columns((pz * NY + py) * ROLES + its_role)
-            peer = group_at(px, py, pz)
-            send(k_in.at[0, :, there], kb.at[i], S_K, peer)
-            send(q_in.at[0, :, there], qb.at[i], S_Q, peer)
-            send(v_in.at[0, :, there], vb.at[i], S_V, peer)
-
-        return carry
-
-    lax.fori_loop(1, GROUP, send_image, 0)
+    for t in range(3):
+
+        def first_hop(n, carry, t=t):
+            i = lax.rem(n, SLOTS_PER_STEP - 1) + 1
+            d = lax.div(n, SLOTS_PER_STEP - 1)
+            px, _, pz = ahead(i)
+            py = lax.rem(y + d, NY)
+
+            @pl.when(role_at(px, py) < ROLES)
+            def _():
+                send(image[t].at[0, :, head_at(px, py, pz)], relay.at[t, d, i], S_HOP + t, group_at(px, y, pz))
+
+            return carry
+
+        lax.fori_loop(0, NY * (SLOTS_PER_STEP - 1), first_hop, 0)
     for d in range(1, REPS):
         send(req, rq.at[d], S_REQ, rep_peer(d))
 
@@ -193,6 +207,16 @@
     place_t[...] = is_place.astype(f32).astype(bf16)
     pick_shift = (sub16 == 2 * request).astype(f32)
     pick_scale = (sub16 == 2 * request + 1).astype(f32)
+
+    def second_hop(t):
+        arrived(relay.at[t, 0:ROLES, 1:SLOTS_PER_STEP], S_HOP + t)
+        for d in (1, 3, 2, 0):
+
+            @pl.when(role_at(x, y + d) < ROLES)
+            def _(d=d):
+                own_hop(t, d).wait()
+                if d > 0:
+                    send(relay.at[t, d], final.at[t, d], S_LAST + NY * t + d, y_peer(d))
 
     arrived(md.at[1:NY], S_MOD)
     arrived(stats.at[1:PLANE], S_STAT)
@@ -214,10 +238,12 @@
         shaped = (tx[d].astype(f32) - mean) * scaled * (1.0 + scale) + shift
         xs[d] = shaped.astype(bf16)
 
+    second_hop(0)
     for part in range(2):
         arrived(w.at[part, 1:NY, half], S_W + part)
         send(w.at[part, 1:NY, half], w.at[part, 1:NY, half], S_WC + part, sibling)
 
+    second_hop(1)
     for part, copy in ((0, own_wk), (1, own_wv)):
         copy.wait()
         arrived(w.at[part, 1:NY, half], S_WC + part)
@@ -234,8 +260,51 @@
                 src = sum_s.at[part, :, head_columns(its_role)]
                 send(src, sum_r.at[part, d], S_SUM + part, x_peer(d))
 
+    second_hop(2)
+
     @pl.when(active)
     def _():
+        over_columns = (((1,), (1,)), ((), ()))
+
+        def flatten(block):
+            return block.astype(f32).reshape(STEP, HEAD_DIM).astype(bf16)
+
+        def image_chunk(c):
+            for t, dst in ((1, kh), (2, vh)):
+                if c > 0:
+                    arrived(final.at[t, c], S_LAST + NY * t + c)
+                dst[...] = flatten((final if c > 0 else relay)[t, c])
+
+            def image_step(b, carry):
+                rows = pl.ds(pl.multiple_of(b * STEP, STEP), STEP)
+                s = lax.dot_general(qh[rows, :], kh[...], over_columns, preferred_element_type=f32)
+                highest = jnp.max(s, axis=1, keepdims=True)
+                if c == 0:
+                    newest = jnp.broadcast_to(highest, (STEP, HEAD_DIM))
+                else:
+                    newest = jnp.maximum(m[rows, :], highest)
+                weights = jnp.exp2((s - newest[:, 0:1]) * FACTOR)
+                total = jnp.sum(weights, axis=1, keepdims=True)
+                mixed = jnp.dot(weights.astype(bf16), vh[...], preferred_element_type=f32)
+                if c == 0:
+                    l[rows, :] = jnp.broadcast_to(total, (STEP, HEAD_DIM))
+                    o[rows, :] = mixed
+                else:
+                    fade = jnp.exp2((m[rows, :] - newest) * FACTOR)
+                    l[rows, :] = l[rows, :] * fade + total
+                    o[rows, :] = o[rows, :] * fade + mixed
+                m[rows, :] = newest
+                return carry
+
+            lax.fori_loop(0, STEPS, image_step, 0)
+
+        for d in (0, 1, 3, 2):
+            if d > 0:
+                arrived(final.at[0, d], S_LAST + d)
+            qh[pl.ds(d * STEP, STEP), :] = flatten((final if d > 0 else relay)[0, d])
+        image_chunk(0)
+        image_chunk(1)
+
         for part in range(2):
             arrived(sum_r.at[part, 1:NX], S_SUM + part)
             rows = acc[part, :, head_columns(role)]
@@ -248,32 +317,8 @@
                 send(src, landed.at[part, d], S_REP + part, rep_peer(d))
             landed[part, 0] = rep_s[part, rep]
 
-        for (src, dst, index), index_all in zip(own_image, (S_K, S_Q, S_V)):
-            pltpu.make_async_copy(src.at[0, :, own_head], dst.at[0], lsem.at[index]).wait()
-            arrived(dst.at[1:GROUP], index_all)
-
-        def flatten(b, carry):
-            slots = pl.ds(b * SLOTS_PER_STEP, SLOTS_PER_STEP)
-            rows = pl.ds(pl.multiple_of(b * STEP, STEP), STEP)
-            for src, dst in ((kb, kh), (qb, qh), (vb, vh)):
-                dst[rows, :] = src[slots].astype(f32).reshape(STEP, HEAD_DIM).astype(bf16)
-            return carry
-
-        lax.fori_loop(0, STEPS, flatten, 0)
-
-        over_columns = (((1,), (1,)), ((), ()))
-
-        def image_step(b, carry):
-            rows = pl.ds(pl.multiple_of(b * STEP, STEP), STEP)
-            s = lax.dot_general(qh[rows, :], kh[...], over_columns, preferred_element_type=f32)
-            highest = jnp.max(s, axis=1, keepdims=True)
-            weights = jnp.exp2((s - highest) * FACTOR)
-            m[rows, :] = jnp.broadcast_to(highest, (STEP, HEAD_DIM))
-            l[rows, :] = jnp.broadcast_to(jnp.sum(weights, axis=1, keepdims=True), (STEP, HEAD_DIM))
-            o[rows, :] = jnp.dot(weights.astype(bf16), vh[...], preferred_element_type=f32)
-            return carry
-
-        lax.fori_loop(0, STEPS, image_step, 0)
+        image_chunk(3)
+        image_chunk(2)
 
         arrived(rq.at[1:REPS], S_REQ)
         named = jnp.concatenate([rq[d] for d in range(REPS)], axis=0) == rep
@@ -314,13 +359,11 @@
             return carry
 
         lax.fori_loop(0, STEPS, text_step, 0)
-        last = pltpu.make_async_copy(o_s.at[0], out.at[0, :, own_head], lsem.at[8])
+        last = pltpu.make_async_copy(o_s.at[0], out.at[0, :, own_head], lsem.at[17])
         last.start()
         arrived(out.at[0, :, 0 : (NY * NZ * ROLES - 1) * HEAD_DIM], S_OUT)
         last.wait()
         left(o_s.at[1:GROUP], S_OUT)
-        for index in (S_K, S_Q, S_V):
-            left(kb.at[1 : NY * NZ * ROLES], index)
         for part in range(2):
             left(sum_r.at[part, 1 : NX - 1], S_SUM + part)
             left(landed.at[part, 1:REPS], S_REP + part)
@@ -329,10 +372,16 @@
     def _():
         arrived(rq.at[1:REPS], S_REQ)
         arrived(out.at[0], S_OUT)
-        for index in (S_K, S_Q, S_V):
-            left(kb.at[0 : NY * NZ * ROLES], index)
         for part in range(2):
             left(sum_r.at[part, 1:NX], S_SUM + part)
+
+    for t in range(3):
+        left(relay.at[t, 0:ROLES, 1:SLOTS_PER_STEP], S_HOP + t)
+        for d in range(1, NY):
+
+            @pl.when(role_at(x, y + d) < ROLES)
+            def _(t=t, d=d):
+                left(relay.at[t, d], S_LAST + NY * t + d)
 
     left(tx.at[1:NY], S_TEXT)
     left(md.at[1:NY], S_MOD)
@@ -349,6 +398,7 @@
     hbm = pl.BlockSpec(memory_space=pl.ANY)
     features = text_rows.shape[1]
     blocks = pltpu.VMEM((GROUP, IMG_DEV, HEAD_DIM), bf16)
+    hops = pltpu.VMEM((3, NY, SLOTS_PER_STEP, IMG_DEV, HEAD_DIM), bf16)
     return pl.pallas_call(
         kernel,
         out_shape=jax.ShapeDtypeStruct(q_image.shape, bf16),
@@ -360,9 +410,8 @@
             pltpu.VMEM((NY, 2 * REPS, features), f32),
             pltpu.VMEM((REPS, 1, ROWS), jnp.int32),
             pltpu.VMEM((2, NY, features, WIDE), bf16),
-            blocks,
-            blocks,
-            blocks,
+            hops,
+            hops,
             pltpu.VMEM((PLANE, 8, ROWS), f32),
             pltpu.VMEM((NY, features, ROWS), bf16),
             pltpu.VMEM((2, ROWS, WIDE), f32),
@@ -372,15 +421,15 @@
             pltpu.VMEM((2, REPS, SLOTS, HEAD_DIM), bf16),
             pltpu.VMEM((2, REPS, SLOTS, HEAD_DIM), bf16),
             pltpu.VMEM((IMG, HEAD_DIM), bf16),
-            pltpu.VMEM((IMG, HEAD_DIM), bf16),
-            pltpu.VMEM((IMG, HEAD_DIM), bf16),
+            pltpu.VMEM((STEP, HEAD_DIM), bf16),
+            pltpu.VMEM((STEP, HEAD_DIM), bf16),
             pltpu.VMEM((IMG, HEAD_DIM), f32),
             pltpu.VMEM((IMG, HEAD_DIM), f32),
             pltpu.VMEM((IMG, HEAD_DIM), f32),
             blocks,
             pltpu.SemaphoreType.DMA((S_ALL,)),
             pltpu.SemaphoreType.DMA((S_ALL,)),
-            pltpu.SemaphoreType.DMA((9,)),
+            pltpu.SemaphoreType.DMA((18,)),
         ],
         compiler_params=pltpu.CompilerParams(
             collective_id=0, has_side_effects=True, vmem_limit_bytes=VMEM_LIMIT

time: 70 us -> 64.7 us (0.924)
  Pallas kernels: 68.1 us -> 62.9 us
    pallas_call x1, Pallas kernels: 68.1 us -> 62.9 us  [local(): pl.pallas_call(kernel, out_shape=jax.ShapeDtypeStruct(q_image.shape, bf16...]
where the time goes in v3:
time: 64.7 us; the launch traced here: 64.6 us
  Pallas kernels  62.9 us (97%)
  local copies, waits for them, and re-layouts  1.73 us (3%)
    pallas_call x1, Pallas kernels, local(): pl.pallas_call(kernel, out_shape=jax.ShapeDtypeStruct(q_image.shape, bf16...  62.9 us
    unnamed x1, local copies, waits for them, and re-layouts  1.73 us

profile of v3, /device:TPU:1, one launch (start us, length us, event | category | flops | bytes accessed | tf_op | source)
XLA Modules:
  0.0 64.6 jit_solution(14626277980061216325)
XLA Ops:
  0.0 62.9 %shard_map.91 = bf16[1,56,3072]{2,1,0:T(8,128)(2,1)} custom-call(bf16[192,256]{1,0:T(8,128)(2,1)} %bitcast.2, f32[50,2,192]{2,1,0:T(2,128)} %mod.1, s32[8]{0:T(128)} %step.1, s32[1,256]{1,0:T(1,128)} %bitcast.3, bf16[192,1536]{1,0:T(8,128)(2,1)} %w_key.1, bf16[192,1536]{1,0:T(8,128)(2,1)} %w_value.1, bf16[1,56,3072]{2,1,0:T(8,128)(2,1)} %q_in.1, ...), custom_call_target="tpu_custom_call" | custom-call | tf_op jit(solution)/shard_map/pallas_call | solution.py:402
  62.9 1.7 %copy.11 = bf16[1,56,3072]{2,1,0:T(8,128)(2,1)} copy(bf16[1,56,3072]{2,1,0:T(8,128)(2,1)} %shard_map.91) | data formatting | bytes 688128

commit v4 on v3

--- a/solution.py
+++ b/solution.py
@@ -23,7 +23,8 @@
 IMG = GROUP * IMG_DEV
 SLOTS_PER_STEP = 8
 STEP = SLOTS_PER_STEP * IMG_DEV
-STEPS = GROUP // SLOTS_PER_STEP
+LANES = 896
+SLOTS_A_STEP = LANES // IMG_DEV
 ROWS = 256
 SLOTS = ROWS // BLOCK * CAP
 TEXT = REPS * SLOTS
@@ -239,11 +240,12 @@
         xs[d] = shaped.astype(bf16)
 
     second_hop(0)
+    second_hop(1)
     for part in range(2):
         arrived(w.at[part, 1:NY, half], S_W + part)
         send(w.at[part, 1:NY, half], w.at[part, 1:NY, half], S_WC + part, sibling)
 
-    second_hop(1)
+    second_hop(2)
     for part, copy in ((0, own_wk), (1, own_wv)):
         copy.wait()
         arrived(w.at[part, 1:NY, half], S_WC + part)
@@ -260,14 +262,27 @@
                 src = sum_s.at[part, :, head_columns(its_role)]
                 send(src, sum_r.at[part, d], S_SUM + part, x_peer(d))
 
-    second_hop(2)
-
     @pl.when(active)
     def _():
         over_columns = (((1,), (1,)), ((), ()))
 
         def flatten(block):
             return block.astype(f32).reshape(STEP, HEAD_DIM).astype(bf16)
+
+        def update(lanes, s, values, first):
+            newest = jnp.max(s, axis=0, keepdims=True)
+            if not first:
+                newest = jnp.maximum(m[:, lanes], newest)
+            weights = jnp.exp2((s - newest) * FACTOR)
+            total = jnp.sum(weights, axis=0, keepdims=True)
+            mixed = lax.dot_general(values, weights.astype(bf16), over_rows, preferred_element_type=f32)
+            if not first:
+                fade = jnp.exp2((m[:, lanes] - newest) * FACTOR)
+                total = l[:, lanes] * fade + total
+                mixed = o[:, lanes] * fade + mixed
+            m[:, lanes] = newest
+            l[:, lanes] = total
+            o[:, lanes] = mixed
 
         def image_chunk(c):
             for t, dst in ((1, kh), (2, vh)):
@@ -276,34 +291,18 @@
                 dst[...] = flatten((final if c > 0 else relay)[t, c])
 
             def image_step(b, carry):
-                rows = pl.ds(pl.multiple_of(b * STEP, STEP), STEP)
-                s = lax.dot_general(qh[rows, :], kh[...], over_columns, preferred_element_type=f32)
-                highest = jnp.max(s, axis=1, keepdims=True)
-                if c == 0:
-                    newest = jnp.broadcast_to(highest, (STEP, HEAD_DIM))
-                else:
-                    newest = jnp.maximum(m[rows, :], highest)
-                weights = jnp.exp2((s - newest[:, 0:1]) * FACTOR)
-                total = jnp.sum(weights, axis=1, keepdims=True)
-                mixed = jnp.dot(weights.astype(bf16), vh[...], preferred_element_type=f32)
-                if c == 0:
-                    l[rows, :] = jnp.broadcast_to(total, (STEP, HEAD_DIM))
-                    o[rows, :] = mixed
-                else:
-                    fade = jnp.exp2((m[rows, :] - newest) * FACTOR)
-                    l[rows, :] = l[rows, :] * fade + total
-                    o[rows, :] = o[rows, :] * fade + mixed
-                m[rows, :] = newest
+                lanes = pl.ds(pl.multiple_of(b * LANES, LANES), LANES)
+                s = lax.dot_general(kh[...], qh[lanes, :], over_columns, preferred_element_type=f32)
+                update(lanes, s, vh[...], c == 0)
                 return carry
 
-            lax.fori_loop(0, STEPS, image_step, 0)
+            lax.fori_loop(0, IMG // LANES, image_step, 0)
 
         for d in (0, 1, 3, 2):
             if d > 0:
                 arrived(final.at[0, d], S_LAST + d)
             qh[pl.ds(d * STEP, STEP), :] = flatten((final if d > 0 else relay)[0, d])
         image_chunk(0)
-        image_chunk(1)
 
         for part in range(2):
             arrived(sum_r.at[part, 1:NX], S_SUM + part)
@@ -317,37 +316,31 @@
                 send(src, landed.at[part, d], S_REP + part, rep_peer(d))
             landed[part, 0] = rep_s[part, rep]
 
+        image_chunk(1)
         image_chunk(3)
         image_chunk(2)
+
 
         arrived(rq.at[1:REPS], S_REQ)
         named = jnp.concatenate([rq[d] for d in range(REPS)], axis=0) == rep
         counted = jnp.sum(jnp.where(named, 1.0, 0.0), axis=1, keepdims=True)
-        lane = lax.broadcasted_iota(jnp.int32, (REPS, TEXT), 1)
-        in_rep = lax.broadcasted_iota(jnp.int32, (REPS, TEXT), 0) == lax.div(lane, SLOTS)
-        bound = jnp.sum(jnp.where(in_rep, counted, 0.0), axis=0, keepdims=True)
-        live = lax.rem(lane, SLOTS)[0:1].astype(f32) < bound
+        slot_number = lax.broadcasted_iota(jnp.int32, (SLOTS, HEAD_DIM), 0).astype(f32)
+        live = jnp.concatenate([slot_number < counted[d : d + 1] for d in range(REPS)], axis=0)
 
         for part in range(2):
             arrived(landed.at[part, 1:REPS], S_REP + part)
 
         def text_step(b, carry):
-            rows = pl.ds(pl.multiple_of(b * STEP, STEP), STEP)
+            lanes = pl.ds(pl.multiple_of(b * LANES, LANES), LANES)
             keys = landed[0].reshape(TEXT, HEAD_DIM)
             values = landed[1].reshape(TEXT, HEAD_DIM)
-            s = lax.dot_general(qh[rows, :], keys, over_columns, preferred_element_type=f32)
-            s = jnp.where(live, s, LOWEST)
-            before = m[rows, :]
-            newest = jnp.maximum(before, jnp.max(s, axis=1, keepdims=True))
-            weights = jnp.exp2((s - newest[:, 0:1]) * FACTOR)
-            fade = jnp.exp2((before - newest) * FACTOR)
-            total = l[rows, :] * fade + jnp.sum(weights, axis=1, keepdims=True)
-            mixed = o[rows, :] * fade + jnp.dot(weights.astype(bf16), values, preferred_element_type=f32)
-            result = (mixed / total).reshape(SLOTS_PER_STEP, IMG_DEV, HEAD_DIM)
-            o_s[pl.ds(b * SLOTS_PER_STEP, SLOTS_PER_STEP)] = result.astype(bf16)
+            s = lax.dot_general(keys, qh[lanes, :], over_columns, preferred_element_type=f32)
+            update(lanes, jnp.where(live[:, 0:1], s, LOWEST), values, False)
+            result = (o[:, lanes] / l[:, lanes]).T.reshape(SLOTS_A_STEP, IMG_DEV, HEAD_DIM)
+            o_s[pl.ds(b * SLOTS_A_STEP, SLOTS_A_STEP)] = result.astype(bf16)
 
             def send_result(k, inner):
-                i = b * SLOTS_PER_STEP + k
+                i = b * SLOTS_A_STEP + k
 
                 @pl.when(i > 0)
                 def _():
@@ -355,10 +348,10 @@
 
                 return inner
 
-            lax.fori_loop(0, SLOTS_PER_STEP, send_result, 0)
+            lax.fori_loop(0, SLOTS_A_STEP, send_result, 0)
             return carry
 
-        lax.fori_loop(0, STEPS, text_step, 0)
+        lax.fori_loop(0, IMG // LANES, text_step, 0)
         last = pltpu.make_async_copy(o_s.at[0], out.at[0, :, own_head], lsem.at[17])
         last.start()
         arrived(out.at[0, :, 0 : (NY * NZ * ROLES - 1) * HEAD_DIM], S_OUT)
@@ -423,9 +416,9 @@
             pltpu.VMEM((IMG, HEAD_DIM), bf16),
             pltpu.VMEM((STEP, HEAD_DIM), bf16),
             pltpu.VMEM((STEP, HEAD_DIM), bf16),
-            pltpu.VMEM((IMG, HEAD_DIM), f32),
-            pltpu.VMEM((IMG, HEAD_DIM), f32),
-            pltpu.VMEM((IMG, HEAD_DIM), f32),
+            pltpu.VMEM((1, IMG), f32),
+            pltpu.VMEM((1, IMG), f32),
+            pltpu.VMEM((HEAD_DIM, IMG), f32),
             blocks,
             pltpu.SemaphoreType.DMA((S_ALL,)),
             pltpu.SemaphoreType.DMA((S_ALL,)),

time: 64.7 us -> 60.6 us (0.937)
  Pallas kernels: 62.9 us -> 58.7 us
    pallas_call x1, Pallas kernels: 62.9 us -> 58.7 us  [local(): pl.pallas_call(kernel, out_shape=jax.ShapeDtypeStruct(q_image.shape, bf16...]
where the time goes in v4:
time: 60.6 us; the launch traced here: 60.5 us
  Pallas kernels  58.7 us (97%)
  local copies, waits for them, and re-layouts  1.73 us (3%)
    pallas_call x1, Pallas kernels, local(): pl.pallas_call(kernel, out_shape=jax.ShapeDtypeStruct(q_image.shape, bf16...  58.7 us
    unnamed x1, local copies, waits for them, and re-layouts  1.73 us

profile of v4, /device:TPU:1, one launch (start us, length us, event | category | flops | bytes accessed | tf_op | source)
XLA Modules:
  0.0 60.5 jit_solution(1061741089194327885)
XLA Ops:
  0.0 58.7 %shard_map.91 = bf16[1,56,3072]{2,1,0:T(8,128)(2,1)} custom-call(bf16[192,256]{1,0:T(8,128)(2,1)} %bitcast.2, f32[50,2,192]{2,1,0:T(2,128)} %mod.1, s32[8]{0:T(128)} %step.1, s32[1,256]{1,0:T(1,128)} %bitcast.3, bf16[192,1536]{1,0:T(8,128)(2,1)} %w_key.1, bf16[192,1536]{1,0:T(8,128)(2,1)} %w_value.1, bf16[1,56,3072]{2,1,0:T(8,128)(2,1)} %q_in.1, ...), custom_call_target="tpu_custom_call" | custom-call | tf_op jit(solution)/shard_map/pallas_call | solution.py:395
  58.7 1.7 %copy.11 = bf16[1,56,3072]{2,1,0:T(8,128)(2,1)} copy(bf16[1,56,3072]{2,1,0:T(8,128)(2,1)} %shard_map.91) | data formatting | bytes 688128

commit v5 on v4

--- a/solution.py
+++ b/solution.py
@@ -240,12 +240,10 @@
         xs[d] = shaped.astype(bf16)
 
     second_hop(0)
-    second_hop(1)
     for part in range(2):
         arrived(w.at[part, 1:NY, half], S_W + part)
         send(w.at[part, 1:NY, half], w.at[part, 1:NY, half], S_WC + part, sibling)
 
-    second_hop(2)
     for part, copy in ((0, own_wk), (1, own_wv)):
         copy.wait()
         arrived(w.at[part, 1:NY, half], S_WC + part)
@@ -261,6 +259,9 @@
             def _(part=part, d=d, its_role=its_role):
                 src = sum_s.at[part, :, head_columns(its_role)]
                 send(src, sum_r.at[part, d], S_SUM + part, x_peer(d))
+
+    second_hop(1)
+    second_hop(2)
 
     @pl.when(active)
     def _():
@@ -330,7 +331,8 @@
         for part in range(2):
             arrived(landed.at[part, 1:REPS], S_REP + part)
 
-        def text_step(b, carry):
+        def text_step(n, carry):
+            b = IMG // LANES - 1 - n
             lanes = pl.ds(pl.multiple_of(b * LANES, LANES), LANES)
             keys = landed[0].reshape(TEXT, HEAD_DIM)
             values = landed[1].reshape(TEXT, HEAD_DIM)
@@ -340,7 +342,7 @@
             o_s[pl.ds(b * SLOTS_A_STEP, SLOTS_A_STEP)] = result.astype(bf16)
 
             def send_result(k, inner):
-                i = b * SLOTS_A_STEP + k
+                i = b * SLOTS_A_STEP + SLOTS_A_STEP - 1 - k
 
                 @pl.when(i > 0)
                 def _():

time: 60.6 us -> 57.7 us (0.952)
  Pallas kernels: 58.7 us -> 55.8 us
    pallas_call x1, Pallas kernels: 58.7 us -> 55.8 us  [local(): pl.pallas_call(kernel, out_shape=jax.ShapeDtypeStruct(q_image.shape, bf16...]
where the time goes in v5:
time: 57.7 us; the launch traced here: 57.6 us
  Pallas kernels  55.8 us (97%)
  local copies, waits for them, and re-layouts  1.73 us (3%)
    pallas_call x1, Pallas kernels, local(): pl.pallas_call(kernel, out_shape=jax.ShapeDtypeStruct(q_image.shape, bf16...  55.8 us
    unnamed x1, local copies, waits for them, and re-layouts  1.73 us

profile of v5, /device:TPU:1, one launch (start us, length us, event | category | flops | bytes accessed | tf_op | source)
XLA Modules:
  0.0 57.6 jit_solution(11291409074384680965)
XLA Ops:
  0.0 55.8 %shard_map.91 = bf16[1,56,3072]{2,1,0:T(8,128)(2,1)} custom-call(bf16[192,256]{1,0:T(8,128)(2,1)} %bitcast.2, f32[50,2,192]{2,1,0:T(2,128)} %mod.1, s32[8]{0:T(128)} %step.1, s32[1,256]{1,0:T(1,128)} %bitcast.3, bf16[192,1536]{1,0:T(8,128)(2,1)} %w_key.1, bf16[192,1536]{1,0:T(8,128)(2,1)} %w_value.1, bf16[1,56,3072]{2,1,0:T(8,128)(2,1)} %q_in.1, ...), custom_call_target="tpu_custom_call" | custom-call | tf_op jit(solution)/shard_map/pallas_call | solution.py:397
  55.9 1.7 %copy.11 = bf16[1,56,3072]{2,1,0:T(8,128)(2,1)} copy(bf16[1,56,3072]{2,1,0:T(8,128)(2,1)} %shard_map.91) | data formatting | bytes 688128

commit v6 on v5

--- a/solution.py
+++ b/solution.py
@@ -28,7 +28,6 @@
 ROWS = 256
 SLOTS = ROWS // BLOCK * CAP
 TEXT = REPS * SLOTS
-HALF = 96
 FACTOR = math.log2(math.e) / math.sqrt(HEAD_DIM)
 LOWEST = -1e30
 VMEM_LIMIT = 60 * 1024 * 1024
@@ -112,13 +111,27 @@
     own = [
         pltpu.make_async_copy(text, tx.at[0], lsem.at[0]),
         pltpu.make_async_copy(mod, mod_v, lsem.at[1]),
-        pltpu.make_async_copy(req, rq.at[0], lsem.at[2]),
-        pltpu.make_async_copy(w_key.at[:, columns(y)], w.at[0, 0], lsem.at[3]),
-        pltpu.make_async_copy(w_value.at[:, columns(y)], w.at[1, 0], lsem.at[4]),
+        pltpu.make_async_copy(req, rq.at[rep], lsem.at[2]),
     ]
-    own_text, own_mod, own_req, own_wk, own_wv = own
+    own_text, own_mod, own_req = own
     for copy in own:
         copy.start()
+
+    core = lax.rem(rep, 2)
+    sibling = (rep + 1 - 2 * core, seq, z)
+    both = rep - core
+
+    def on_core(number, src, what):
+        @pl.when(core == number)
+        def _():
+            what(src)
+
+    def own_weights(src):
+        return pltpu.make_async_copy(src.at[:, columns(y)], w.at[0], lsem.at[3])
+
+    on_core(0, w_key, lambda src: own_weights(src).start())
+    on_core(1, w_value, lambda src: own_weights(src).start())
+
     def role_at(px, py):
         return lax.rem(px + py, NX)
 
@@ -169,13 +182,12 @@
 
     lax.fori_loop(1, PLANE, send_stats, 0)
 
-    core = lax.rem(rep, 2)
-    sibling = (rep + 1 - 2 * core, seq, z)
-    half = pl.ds(pl.multiple_of(core * HALF, HALF), HALF)
-    for part, src in ((0, w_key), (1, w_value)):
+    def send_weights(src):
         for d in range(1, NY):
-            there = columns(lax.rem(y + d, NY))
-            send(src.at[half, there], w.at[part, d, half], S_W + part, y_peer(d))
+            send(src.at[:, columns(lax.rem(y + d, NY))], w.at[d], S_W, y_peer(d))
+
+    on_core(0, w_key, send_weights)
+    on_core(1, w_value, send_weights)
 
     for t in range(3):
 
@@ -193,19 +205,11 @@
 
         lax.fori_loop(0, NY * (SLOTS_PER_STEP - 1), first_hop, 0)
     for d in range(1, REPS):
-        send(req, rq.at[d], S_REQ, rep_peer(d))
+        send(req, rq.at[rep], S_REQ, rep_peer(d))
 
     own_req.wait()
-    request = rq[0]
+    request = rq[rep]
     sub16 = lax.broadcasted_iota(jnp.int32, (16, ROWS), 0)
-    is_target = sub16 == request
-    first_row = lax.broadcasted_iota(jnp.int32, (ROWS, ROWS), 0)
-    second_row = lax.broadcasted_iota(jnp.int32, (ROWS, ROWS), 1)
-    earlier = (first_row < second_row).astype(f32).astype(bf16)
-    count = jnp.dot(is_target.astype(f32).astype(bf16), earlier, preferred_element_type=f32)
-    slot = jnp.sum(jnp.where(is_target, count, 0.0), axis=0, keepdims=True).astype(jnp.int32)
-    is_place = lax.broadcasted_iota(jnp.int32, (TEXT, ROWS), 0) == request * SLOTS + slot
-    place_t[...] = is_place.astype(f32).astype(bf16)
     pick_shift = (sub16 == 2 * request).astype(f32)
     pick_scale = (sub16 == 2 * request + 1).astype(f32)
 
@@ -237,18 +241,17 @@
             md[d], pick_scale, over_rows, precision=lax.Precision.HIGHEST, preferred_element_type=f32
         )
         shaped = (tx[d].astype(f32) - mean) * scaled * (1.0 + scale) + shift
-        xs[d] = shaped.astype(bf16)
+        xs[core, d] = shaped.astype(bf16)
+    send(xs.at[core], xs.at[core], S_WC, sibling)
 
     second_hop(0)
+    arrived(w.at[1:NY], S_W)
+    on_core(0, w_key, lambda src: own_weights(src).wait())
+    on_core(1, w_value, lambda src: own_weights(src).wait())
+    arrived(xs.at[0], S_WC)
     for part in range(2):
-        arrived(w.at[part, 1:NY, half], S_W + part)
-        send(w.at[part, 1:NY, half], w.at[part, 1:NY, half], S_WC + part, sibling)
-
-    for part, copy in ((0, own_wk), (1, own_wv)):
-        copy.wait()
-        arrived(w.at[part, 1:NY, half], S_WC + part)
         acc[part] = lax.dot_general(
-            xs[...].reshape(D // NX, ROWS), w[part].reshape(D // NX, WIDE), over_rows,
+            xs[part].reshape(D // NX, ROWS), w[...].reshape(D // NX, WIDE), over_rows,
             preferred_element_type=f32,
         )
         sum_s[part] = acc[part].astype(bf16)
@@ -262,6 +265,18 @@
 
     second_hop(1)
     second_hop(2)
+
+    arrived(rq.at[1:REPS], S_REQ)
+    first_row = lax.broadcasted_iota(jnp.int32, (ROWS, ROWS), 0)
+    second_row = lax.broadcasted_iota(jnp.int32, (ROWS, ROWS), 1)
+    earlier = (first_row < second_row).astype(f32).astype(bf16)
+    for part in range(2):
+        request = rq[both + part]
+        is_target = sub16 == request
+        count = jnp.dot(is_target.astype(f32).astype(bf16), earlier, preferred_element_type=f32)
+        slot = jnp.sum(jnp.where(is_target, count, 0.0), axis=0, keepdims=True).astype(jnp.int32)
+        is_place = lax.broadcasted_iota(jnp.int32, (TEXT, ROWS), 0) == request * SLOTS + slot
+        place_t[part] = is_place.astype(f32).astype(bf16)
 
     @pl.when(active)
     def _():
@@ -303,33 +318,31 @@
             if d > 0:
                 arrived(final.at[0, d], S_LAST + d)
             qh[pl.ds(d * STEP, STEP), :] = flatten((final if d > 0 else relay)[0, d])
-        image_chunk(0)
 
         for part in range(2):
             arrived(sum_r.at[part, 1:NX], S_SUM + part)
             rows = acc[part, :, head_columns(role)]
             for d in range(1, NX):
                 rows = rows + sum_r[part, d].astype(f32)
-            moved = jnp.dot(place_t[...], rows.astype(bf16), preferred_element_type=f32)
+            moved = jnp.dot(place_t[part], rows.astype(bf16), preferred_element_type=f32)
             rep_s[part] = moved.astype(bf16).reshape(REPS, SLOTS, HEAD_DIM)
             for d in range(1, REPS):
                 src = rep_s.at[part, lax.rem(rep + d, REPS)]
-                send(src, landed.at[part, d], S_REP + part, rep_peer(d))
-            landed[part, 0] = rep_s[part, rep]
-
+                send(src, landed.at[core, both + part], S_REP, rep_peer(d))
+            landed[core, both + part] = rep_s[part, rep]
+
+        image_chunk(0)
+        image_chunk(3)
         image_chunk(1)
-        image_chunk(3)
         image_chunk(2)
 
 
-        arrived(rq.at[1:REPS], S_REQ)
         named = jnp.concatenate([rq[d] for d in range(REPS)], axis=0) == rep
         counted = jnp.sum(jnp.where(named, 1.0, 0.0), axis=1, keepdims=True)
         slot_number = lax.broadcasted_iota(jnp.int32, (SLOTS, HEAD_DIM), 0).astype(f32)
         live = jnp.concatenate([slot_number < counted[d : d + 1] for d in range(REPS)], axis=0)
 
-        for part in range(2):
-            arrived(landed.at[part, 1:REPS], S_REP + part)
+        arrived(landed.at[0:2, 1:REPS], S_REP)
 
         def text_step(n, carry):
             b = IMG // LANES - 1 - n
@@ -361,11 +374,10 @@
         left(o_s.at[1:GROUP], S_OUT)
         for part in range(2):
             left(sum_r.at[part, 1 : NX - 1], S_SUM + part)
-            left(landed.at[part, 1:REPS], S_REP + part)
+        left(landed.at[0:2, 1:REPS], S_REP)
 
     @pl.when(idle)
     def _():
-        arrived(rq.at[1:REPS], S_REQ)
         arrived(out.at[0], S_OUT)
         for part in range(2):
             left(sum_r.at[part, 1:NX], S_SUM + part)
@@ -382,9 +394,8 @@
     left(md.at[1:NY], S_MOD)
     left(stats.at[1:PLANE], S_STAT)
     left(rq.at[1:REPS], S_REQ)
-    for part in range(2):
-        left(w.at[part, 1:NY, half], S_W + part)
-        left(w.at[part, 1:NY, half], S_WC + part)
+    left(w.at[1:NY], S_W)
+    left(xs.at[0], S_WC)
 
 
 def local(text_rows, modulation, timestep, row_request, w_key, w_value, q_image, k_image, v_image):
@@ -404,15 +415,15 @@
             pltpu.VMEM(modulation.shape, f32),
             pltpu.VMEM((NY, 2 * REPS, features), f32),
             pltpu.VMEM((REPS, 1, ROWS), jnp.int32),
-            pltpu.VMEM((2, NY, features, WIDE), bf16),
+            pltpu.VMEM((NY, features, WIDE), bf16),
             hops,
             hops,
             pltpu.VMEM((PLANE, 8, ROWS), f32),
-            pltpu.VMEM((NY, features, ROWS), bf16),
+            pltpu.VMEM((2, NY, features, ROWS), bf16),
             pltpu.VMEM((2, ROWS, WIDE), f32),
             pltpu.VMEM((2, ROWS, WIDE), bf16),
             pltpu.VMEM((2, NX, ROWS, HEAD_DIM), bf16),
-            pltpu.VMEM((TEXT, ROWS), bf16),
+            pltpu.VMEM((2, TEXT, ROWS), bf16),
             pltpu.VMEM((2, REPS, SLOTS, HEAD_DIM), bf16),
             pltpu.VMEM((2, REPS, SLOTS, HEAD_DIM), bf16),
             pltpu.VMEM((IMG, HEAD_DIM), bf16),

time: 57.7 us -> 56.5 us (0.979)
  Pallas kernels: 55.8 us -> 54.5 us
    pallas_call x1, Pallas kernels: 55.8 us -> 54.5 us  [local(): pl.pallas_call(kernel, out_shape=jax.ShapeDtypeStruct(q_image.shape, bf16...]
where the time goes in v6:
time: 56.5 us; the launch traced here: 56.3 us
  Pallas kernels  54.5 us (96%)
  local copies, waits for them, and re-layouts  1.73 us (3%)
    pallas_call x1, Pallas kernels, local(): pl.pallas_call(kernel, out_shape=jax.ShapeDtypeStruct(q_image.shape, bf16...  54.5 us
    unnamed x1, local copies, waits for them, and re-layouts  1.73 us

profile of v6, /device:TPU:1, one launch (start us, length us, event | category | flops | bytes accessed | tf_op | source)
XLA Modules:
  0.0 56.3 jit_solution(8529219096850353057)
XLA Ops:
  0.0 54.5 %shard_map.91 = bf16[1,56,3072]{2,1,0:T(8,128)(2,1)} custom-call(bf16[192,256]{1,0:T(8,128)(2,1)} %bitcast.2, f32[50,2,192]{2,1,0:T(2,128)} %mod.1, s32[8]{0:T(128)} %step.1, s32[1,256]{1,0:T(1,128)} %bitcast.3, bf16[192,1536]{1,0:T(8,128)(2,1)} %w_key.1, bf16[192,1536]{1,0:T(8,128)(2,1)} %w_value.1, bf16[1,56,3072]{2,1,0:T(8,128)(2,1)} %q_in.1, ...), custom_call_target="tpu_custom_call" | custom-call | tf_op jit(solution)/shard_map/pallas_call | solution.py:408
  54.5 1.7 %copy.11 = bf16[1,56,3072]{2,1,0:T(8,128)(2,1)} copy(bf16[1,56,3072]{2,1,0:T(8,128)(2,1)} %shard_map.91) | data formatting | bytes 688128

commit v7 on v6

--- a/solution.py
+++ b/solution.py
@@ -182,6 +182,9 @@
 
     lax.fori_loop(1, PLANE, send_stats, 0)
 
+    for d in range(1, REPS):
+        send(req, rq.at[rep], S_REQ, rep_peer(d))
+
     def send_weights(src):
         for d in range(1, NY):
             send(src.at[:, columns(lax.rem(y + d, NY))], w.at[d], S_W, y_peer(d))
@@ -204,8 +207,6 @@
             return carry
 
         lax.fori_loop(0, NY * (SLOTS_PER_STEP - 1), first_hop, 0)
-    for d in range(1, REPS):
-        send(req, rq.at[rep], S_REQ, rep_peer(d))
 
     own_req.wait()
     request = rq[rep]

time: 56.5 us -> 56.5 us (level)
  no operation moved by 1% of the time
where the time goes in v7:
time: 56.5 us; the launch traced here: 56.3 us
  Pallas kernels  54.5 us (96%)
  local copies, waits for them, and re-layouts  1.73 us (3%)
    pallas_call x1, Pallas kernels, local(): pl.pallas_call(kernel, out_shape=jax.ShapeDtypeStruct(q_image.shape, bf16...  54.5 us
    unnamed x1, local copies, waits for them, and re-layouts  1.73 us

profile of v7, /device:TPU:1, one launch (start us, length us, event | category | flops | bytes accessed | tf_op | source)
XLA Modules:
  0.0 56.3 jit_solution(13945952466422923124)
XLA Ops:
  0.0 54.5 %shard_map.91 = bf16[1,56,3072]{2,1,0:T(8,128)(2,1)} custom-call(bf16[192,256]{1,0:T(8,128)(2,1)} %bitcast.2, f32[50,2,192]{2,1,0:T(2,128)} %mod.1, s32[8]{0:T(128)} %step.1, s32[1,256]{1,0:T(1,128)} %bitcast.3, bf16[192,1536]{1,0:T(8,128)(2,1)} %w_key.1, bf16[192,1536]{1,0:T(8,128)(2,1)} %w_value.1, bf16[1,56,3072]{2,1,0:T(8,128)(2,1)} %q_in.1, ...), custom_call_target="tpu_custom_call" | custom-call | tf_op jit(solution)/shard_map/pallas_call | solution.py:409
  54.5 1.7 %copy.11 = bf16[1,56,3072]{2,1,0:T(8,128)(2,1)} copy(bf16[1,56,3072]{2,1,0:T(8,128)(2,1)} %shard_map.91) | data formatting | bytes 688128
